TPU v7x, 256 devices: a whole 4x4x8 slice. The times are simulated.
256 devices in a mesh: rep: 16 (over x, y), fsdp: 16 (over z, core).
Axes of the slice: x: 4, y: 4, z: 8, core: 2. Of those that a mesh axis runs over, the one named last changes fastest.
Arguments:
- grads: bfloat16 [256, 704, 1024], P(None, 'fsdp', 'rep')
- momentum: bfloat16 [256, 2, 704, 1024], P(('rep', 'fsdp')), may hold values from -6 to 6
- owner: int32 [256], replicated, may hold values from 0 to 255, as said below
Outputs:
- update: bfloat16 [256, 704, 1024], P(None, 'fsdp', 'rep')
- new_momentum: bfloat16 [256, 2, 704, 1024], P(('rep', 'fsdp'))
Inputs may be any that keep to these rules, and one draw needn't show every extreme that they name: `owner`: every device owns at most 2 matrices, and some device owns exactly 2.
All inputs are finite; a program needn't handle non-finite values.
Results may differ from a plain program's by a relative error of at most 0.0066.
Values may be sent and summed in bfloat16 or wider, within the bound.
A program may use at most 128 MiB of HBM per device.

v0:
```python
import jax
import jax.numpy as jnp
from jax import lax
from jax.sharding import PartitionSpec as P

HID = 704
D = 1024
ITERS = 2


def slots_of(owner):
    order = jnp.arange(owner.shape[0], dtype=jnp.int32)
    earlier = (owner[:, None] == owner[None, :]) & (order[None, :] < order[:, None])
    return jnp.sum(earlier.astype(jnp.int32), axis=1)


def orthogonalize(grad, previous):
    moment = (0.95 * previous.astype(jnp.float32) + grad.astype(jnp.float32)).astype(jnp.bfloat16)
    nesterov = grad.astype(jnp.float32) + 0.95 * lax.optimization_barrier(moment).astype(
        jnp.float32
    )
    total = jnp.sum(nesterov * nesterov, axis=(1, 2), keepdims=True)
    current = (nesterov / (jnp.sqrt(total) + 1e-07)).astype(jnp.bfloat16)
    for turn in range(ITERS):
        gram = jnp.einsum(
            "cik,cjk->cij", current, current, preferred_element_type=jnp.float32
        ).astype(jnp.bfloat16)
        square = jnp.einsum("cik,ckj->cij", gram, gram, preferred_element_type=jnp.float32)
        mixed = (
            -4.775 * lax.optimization_barrier(gram).astype(jnp.float32) + 2.0315 * square
        ).astype(jnp.bfloat16)
        product = jnp.einsum("cik,ckj->cij", mixed, current, preferred_element_type=jnp.float32)
        current = (3.4445 * lax.optimization_barrier(current).astype(jnp.float32) + product).astype(
            jnp.bfloat16
        )
    factor = 0.2 * max(HID, D) ** 0.5
    result = (factor * lax.optimization_barrier(current).astype(jnp.float32)).astype(jnp.bfloat16)
    return (result, moment)


def maybe_orthogonalize(active, grad, previous):

    def run_it(operands):
        return orthogonalize(operands[0], operands[1])

    def skip_it(operands):
        return (jnp.zeros_like(operands[0]), operands[1])

    return lax.cond(active, run_it, skip_it, (grad, previous))


def on_device(grads, momentum, owner):
    fsdp_count = lax.axis_size("fsdp")
    rep_count = lax.axis_size("rep")
    device_count = fsdp_count * rep_count
    matrix_count, tile_rows, tile_cols = grads.shape
    full_rows = fsdp_count * tile_rows
    full_cols = rep_count * tile_cols
    own_index = lax.axis_index("rep") * fsdp_count + lax.axis_index("fsdp")
    slot = slots_of(owner)
    mine = momentum[0]
    capacity = momentum.shape[1]
    flat_index = owner * capacity + slot
    inverse = jnp.full((device_count * capacity,), matrix_count, jnp.int32)
    inverse = inverse.at[flat_index].set(jnp.arange(matrix_count, dtype=jnp.int32))
    padded = jnp.concatenate([grads, jnp.zeros((1, tile_rows, tile_cols), grads.dtype)], axis=0)
    picked = padded[inverse].reshape(rep_count, fsdp_count, capacity, tile_rows, tile_cols)
    picked = picked.transpose(2, 1, 3, 0, 4)
    received = lax.all_to_all(
        lax.all_to_all(picked, "rep", split_axis=3, concat_axis=3, tiled=True),
        "fsdp",
        split_axis=1,
        concat_axis=1,
        tiled=True,
    )
    whole = received.reshape(capacity, full_rows, full_cols)
    own_load = jnp.sum((owner == own_index).astype(jnp.int32))
    results = []
    moments = []
    for position in range(capacity):
        part_result, part_moment = maybe_orthogonalize(
            own_load > position, whole[position : position + 1], mine[position : position + 1]
        )
        results.append(part_result)
        moments.append(part_moment)
    result = jnp.concatenate(results, axis=0)
    new_slots = jnp.concatenate(moments, axis=0)
    outgoing = result.reshape(capacity, fsdp_count, tile_rows, rep_count, tile_cols)
    returned = lax.all_to_all(
        lax.all_to_all(outgoing, "rep", split_axis=3, concat_axis=3, tiled=True),
        "fsdp",
        split_axis=1,
        concat_axis=1,
        tiled=True,
    )
    table = returned.transpose(3, 1, 0, 2, 4).reshape(device_count * capacity, tile_rows, tile_cols)
    update = table[flat_index]
    return (update, new_slots[None])


def solution(mesh):
    return jax.shard_map(
        on_device,
        mesh=mesh,
        in_specs=(P(None, "fsdp", "rep"), P(("rep", "fsdp"), None, None, None), P()),
        out_specs=(P(None, "fsdp", "rep"), P(("rep", "fsdp"), None, None, None)),
        check_vma=False,
    )
```

profile of v0, /device:TPU:1, one launch (start us, length us, event | category | flops | bytes accessed | tf_op | source)
XLA Modules:
  0.0 477.9 jit_solution(8394800321853762151)
XLA Ops:
  4.3 5.2 %copy.33 = bf16[256,44,64]{2,1,0:T(8,128)(2,1)} copy(bf16[256,44,64]{0,2,1:T(8,128)(2,1)} %param.7) | data formatting | bytes 2883584 | tf_op args[0]
  20.5 6.3 %copy.49 = bf16[2,16,44,16,64]{4,0,1,2,3:T(2,128)(2,1)} copy(bf16[2,16,44,16,64]{4,0,1,3,2:T(2,128)(2,1)S(1)} %bitcast.133) | data formatting | bytes 5767168 | tf_op jit(solution)/shard_map/transpose | solution.py:68
  26.8 10.9 %reshape.162 = bf16[16,2,45056]{2,1,0:T(2,128)(2,1)S(1)} reshape(bf16[16,44,16,2,64]{4,3,2,1,0:T(2,128)(2,1)} %bitcast.134) | data formatting | bytes 5767168
  37.8 42.8 %all_to_all.20 = bf16[16,2,45056]{2,1,0:T(2,128)(2,1)} all-to-all(bf16[16,2,45056]{2,1,0:T(2,128)(2,1)S(1)} %reshape.162), channel_id=1, replica_groups=mesh['rep'=16,'fsdp'=16] {'rep'}, dimensions={0} | all-to-all | bytes 5767168 | tf_op jit(solution)/shard_map/all_to_all | solution.py:70
  80.5 12.1 %reshape.163 = bf16[16,44,16,2,64]{4,3,2,1,0:T(2,128)(2,1)} reshape(bf16[16,2,45056]{2,1,0:T(2,128)(2,1)} %all_to_all.20) | data formatting | bytes 5767168
  92.6 7.4 %copy_bitcast_fusion.2 = bf16[16,44,16,2,64]{4,3,2,1,0:T(2,128)(2,1)} fusion(bf16[16,44,16,2,64]{4,3,2,1,0:T(2,128)(2,1)} %reshape.163), kind=kLoop, calls=%fused_computation.73 | loop fusion | bytes 5767168
  100.0 12.4 %reshape.164 = bf16[16,2,45056]{2,1,0:T(2,128)(2,1)} reshape(bf16[16,44,16,2,64]{4,3,2,1,0:T(2,128)(2,1)} %copy_bitcast_fusion.2) | data formatting | bytes 5767168
  112.4 10.9 %all-to-all-start.1 = ((bf16[16,2,45056]{2,1,0:T(2,128)(2,1)}), bf16[16,2,45056]{2,1,0:T(2,128)(2,1)S(1)}, u32[]{:S(2)}, u32[]{:S(2)}) async-start(bf16[16,2,45056]{2,1,0:T(2,128)(2,1)} %reshape.164), calls=%async_computation.1 | async-start | bytes 5767168 | tf_op jit(solution)/shard_map/all_to_all | solution.py:69
  128.3 60.4 %all-to-all-done.1 = bf16[16,2,45056]{2,1,0:T(2,128)(2,1)S(1)} async-done(((bf16[16,2,45056]{2,1,0:T(2,128)(2,1)}), bf16[16,2,45056]{2,1,0:T(2,128)(2,1)S(1)}, u32[]{:S(2)}, u32[]{:S(2)}) %all-to-all-start.1) | async-done | bytes 2883616 | tf_op jit(solution)/shard_map/all_to_all | solution.py:69
  188.7 8.4 %reshape.165 = bf16[16,44,16,2,64]{4,3,2,1,0:T(2,128)(2,1)} reshape(bf16[16,2,45056]{2,1,0:T(2,128)(2,1)S(1)} %all-to-all-done.1) | data formatting | bytes 5767168
  197.1 34.8 %conditional.2 = (bf16[1,704,1024]{2,1,0:T(8,128)(2,1)}, bf16[1,704,1024]{2,1,0:T(8,128)(2,1)}) conditional(s32[]{:T(128)} %convert_element_type.147, bf16[1,704,1024]{2,1,0:T(8,128)(2,1)} %get-tuple-element.52, (bf16[2,16,44,16,64]{4,0,3,2,1:T(2,128)(2,1)}, bf16[1,704,1024]{2,1,0:T(8,128)(2,1)}) %tuple.45), branch_computations={%region_3.0_spmd, %region_4.0_spmd} | conditional | flops 5480431616 | bytes 54968392 | solution.py:49
  235.7 5.8 %reshape.129 = bf16[2,16,44,16,64]{4,3,2,1,0:T(8,128)(2,1)} reshape(bf16[2,704,1024]{2,1,0:T(8,128)(2,1)S(1)} %pad_maximum_fusion) | data formatting | bytes 5767168 | tf_op jit(solution)/shard_map/reshape | solution.py:88
  241.5 11.8 %copy.48 = bf16[2,16,44,16,64]{4,0,1,2,3:T(2,128)(2,1)} copy(bf16[2,16,44,16,64]{4,3,2,1,0:T(8,128)(2,1)} %reshape.129) | data formatting | bytes 5767168 | tf_op jit(solution)/shard_map/reshape | solution.py:88
  253.2 10.9 %reshape.166 = bf16[16,2,45056]{2,1,0:T(2,128)(2,1)S(1)} reshape(bf16[16,44,16,2,64]{4,3,2,1,0:T(2,128)(2,1)} %bitcast.135) | data formatting | bytes 5767168
  264.2 71.4 %all_to_all.21 = bf16[16,2,45056]{2,1,0:T(2,128)(2,1)} all-to-all(bf16[16,2,45056]{2,1,0:T(2,128)(2,1)S(1)} %reshape.166), channel_id=1, replica_groups=mesh['rep'=16,'fsdp'=16] {'rep'}, dimensions={0} | all-to-all | bytes 5767168 | tf_op jit(solution)/shard_map/all_to_all | solution.py:90
  335.5 12.1 %reshape.167 = bf16[16,44,16,2,64]{4,3,2,1,0:T(2,128)(2,1)} reshape(bf16[16,2,45056]{2,1,0:T(2,128)(2,1)} %all_to_all.21) | data formatting | bytes 5767168
  347.6 7.4 %copy_bitcast_fusion = bf16[16,44,16,2,64]{4,3,2,1,0:T(2,128)(2,1)} fusion(bf16[16,44,16,2,64]{4,3,2,1,0:T(2,128)(2,1)} %reshape.167), kind=kLoop, calls=%fused_computation.71 | loop fusion | bytes 5767168
  355.0 12.4 %reshape.168 = bf16[16,2,45056]{2,1,0:T(2,128)(2,1)} reshape(bf16[16,44,16,2,64]{4,3,2,1,0:T(2,128)(2,1)} %copy_bitcast_fusion) | data formatting | bytes 5767168
  367.4 7.5 %all-to-all-start.3 = ((bf16[16,2,45056]{2,1,0:T(2,128)(2,1)}), bf16[16,2,45056]{2,1,0:T(2,128)(2,1)}, u32[]{:S(2)}, u32[]{:S(2)}) async-start(bf16[16,2,45056]{2,1,0:T(2,128)(2,1)} %reshape.168), calls=%async_computation.3 | async-start | bytes 5767168 | tf_op jit(solution)/shard_map/all_to_all | solution.py:89
  376.7 63.6 %all-to-all-done.3 = bf16[16,2,45056]{2,1,0:T(2,128)(2,1)} async-done(((bf16[16,2,45056]{2,1,0:T(2,128)(2,1)}), bf16[16,2,45056]{2,1,0:T(2,128)(2,1)}, u32[]{:S(2)}, u32[]{:S(2)}) %all-to-all-start.3) | async-done | bytes 2883616 | tf_op jit(solution)/shard_map/all_to_all | solution.py:89
  440.3 12.1 %reshape.169 = bf16[16,44,16,2,64]{4,3,2,1,0:T(2,128)(2,1)} reshape(bf16[16,2,45056]{2,1,0:T(2,128)(2,1)} %all-to-all-done.3) | data formatting | bytes 5767168
  452.4 6.1 %bitcast_bitcast_fusion = bf16[16,16,2,44,64]{4,2,0,3,1:T(2,128)(2,1)S(1)} fusion(bf16[16,44,16,2,64]{4,3,2,1,0:T(2,128)(2,1)} %reshape.169), kind=kLoop, calls=%fused_computation.70 | loop fusion | bytes 5767168 | tf_op jit(solution)/shard_map/transpose | solution.py:96
  458.5 5.5 %copy.41 = bf16[16,16,2,44,64]{4,2,1,0,3:T(2,128)(2,1)S(1)} copy(bf16[16,16,2,44,64]{4,2,0,3,1:T(2,128)(2,1)S(1)} %bitcast_bitcast_fusion) | data formatting | bytes 5767168 | tf_op jit(solution)/shard_map/transpose | solution.py:96
  464.0 6.4 %copy.42 = bf16[512,44,64]{2,1,0:T(8,128)(2,1)} copy(bf16[512,44,64]{2,0,1:T(8,128)(2,1)S(1)} %bitcast.136) | data formatting | bytes 5767168 | tf_op jit(solution)/shard_map/reshape | solution.py:96
  (34 shorter events, 66.3 us)
Async XLA Ops:
  112.4 76.3 %all-to-all-start.1 = ((bf16[16,2,45056]{2,1,0:T(2,128)(2,1)}), bf16[16,2,45056]{2,1,0:T(2,128)(2,1)S(1)}, u32[]{:S(2)}, u32[]{:S(2)}) async-start(bf16[16,2,45056]{2,1,0:T(2,128)(2,1)} %reshape.164), calls=%async_computation.1 | async-start | bytes 5767168 | tf_op jit(solution)/shard_map/all_to_all | solution.py:69
  216.9 1.4 copy-start.2
  367.4 7.5 %copy-start = (bf16[1,704,1024]{2,1,0:T(8,128)(2,1)S(1)}, bf16[1,704,1024]{2,1,0:T(8,128)(2,1)}, u32[]{:S(2)}) copy-start(bf16[1,704,1024]{2,1,0:T(8,128)(2,1)} %get-tuple-element.27) | copy-start | bytes 4325380
  367.4 7.5 %copy-start.1 = (bf16[1,704,1024]{2,1,0:T(8,128)(2,1)S(1)}, bf16[1,704,1024]{2,1,0:T(8,128)(2,1)}, u32[]{:S(2)}) copy-start(bf16[1,704,1024]{2,1,0:T(8,128)(2,1)} %get-tuple-element.26) | copy-start | bytes 4325380
  367.4 72.9 %all-to-all-start.3 = ((bf16[16,2,45056]{2,1,0:T(2,128)(2,1)}), bf16[16,2,45056]{2,1,0:T(2,128)(2,1)}, u32[]{:S(2)}, u32[]{:S(2)}) async-start(bf16[16,2,45056]{2,1,0:T(2,128)(2,1)} %reshape.168), calls=%async_computation.3 | async-start | bytes 5767168 | tf_op jit(solution)/shard_map/all_to_all | solution.py:89
where the time goes:
time: 487 us; the launch traced here: 478 us
  local copies, waits for them, and re-layouts  186 us (38%)
  waiting for transfers between devices  124 us (25%)
  blocking collectives  114 us (23%)
  other arithmetic  18.4 us (4%)
  starting transfers between devices  18.4 us (4%)
  matrix products  13.5 us (3%)
    unnamed x16, local copies, waits for them, and re-layouts  114 us
    all_to_all x1, blocking collectives, on_device(): lax.all_to_all(outgoing, 'rep', split_axis=3, concat_axis=3, tiled=True)  71.4 us
    all_to_all x1, waiting for transfers between devices, on_device(): lax.all_to_all(lax.all_to_all(outgoing, 'rep', split_axis=3, concat_axis=...  63.6 us
    all_to_all x1, waiting for transfers between devices, on_device(): lax.all_to_all(lax.all_to_all(picked, 'rep', split_axis=3, concat_axis=3,...  60.4 us
    all_to_all x1, blocking collectives, on_device(): lax.all_to_all(picked, 'rep', split_axis=3, concat_axis=3, tiled=True)  42.8 us
    reshape x2, local copies, waits for them, and re-layouts, on_device(): result.reshape(capacity, fsdp_count, tile_rows, rep_count, tile_cols)  17.6 us
    transpose x2, local copies, waits for them, and re-layouts, on_device(): returned.transpose(3, 1, 0, 2, 4)  11.6 us
    all_to_all x1, starting transfers between devices, on_device(): lax.all_to_all(lax.all_to_all(picked, 'rep', split_axis=3, concat_axis=3,...  10.9 us
  transfers between devices with their start and end apart: 2, of which 2 were waited for; matrix products, arithmetic and copies ran while one was open for 1% of the time, Pallas kernels for 0%

commit v1 on v0

v1 whole, which is shorter than its diff:
```python
import functools

import jax
import jax.numpy as jnp
import numpy as np
from jax import lax
from jax.experimental import pallas as pl
from jax.experimental.pallas import tpu as pltpu
from jax.sharding import PartitionSpec as P

ITERS = 2
MESH = pl.DeviceIdType.MESH
BF = jnp.bfloat16
F32 = jnp.float32


def mm(a, b, dims=((1,), (0,))):
    return lax.dot_general(a, b, (dims, ((), ())), preferred_element_type=F32)


def wait_bytes(ref, sem):
    pltpu.make_async_copy(ref, ref, sem).wait()


def tile_cols(n, size):
    return pl.ds(pl.multiple_of(n * size, size), size)


def kernel(
    cfg,
    owner_ref, g_hbm, mom_hbm, regroup_hbm, regroup_t_hbm, rows_hbm, rows_t_hbm, swap_hbm,
    upd_ref, new_hbm,
    g, regroup, regroup_t, rows, rows_t, swap, keys,
    s_buf, t_buf, v_buf, w_buf, u_buf, mom, new, zp, nest, x, gram, mixed,
    load_sem, mom_sem, new_sem, in_send, in_recv, out_send, out_recv,
):
    nr, nf, half, hid, width, pad = cfg
    rep, fs = lax.axis_index("rep"), lax.axis_index("fsdp")
    mats = nr * nf
    blk = half + 2
    upper = nf * blk

    loads = [(g_hbm, g), (regroup_hbm, regroup), (swap_hbm, swap), (rows_hbm, rows),
             (rows_t_hbm, rows_t), (regroup_t_hbm, regroup_t)]
    loads = [pltpu.make_async_copy(a, b, load_sem.at[i]) for i, (a, b) in enumerate(loads)]
    for load in loads:
        load.start()
    for s in range(2):
        pltpu.make_async_copy(mom_hbm.at[s], mom.at[s], mom_sem.at[s]).start()

    def others(first, last, visit):
        @pl.loop(first, last)
        def _(k):
            to_f = lax.rem(fs + k, nf)

            @pl.loop(0, nr)
            def _(j):
                visit(lax.rem(rep + j, nr), to_f)

    def own_row(visit):
        @pl.loop(1, nr)
        def _(j):
            visit(lax.rem(rep + j, nr), fs)

    barrier = pltpu.get_barrier_semaphore()

    def greet(to_r, to_f):
        pl.semaphore_signal(barrier, inc=1, device_id=(to_r, to_f), device_id_type=MESH)

    own_row(greet)
    others(1, nf, greet)

    owner = owner_ref[...]
    down = jnp.transpose(jnp.broadcast_to(owner, (mats, mats)))
    index = lax.broadcasted_iota(jnp.int32, (mats, mats), 0)
    order = lax.broadcasted_iota(jnp.int32, (mats, mats), 1)
    earlier = jnp.where((down == owner) & (index < order), 1, 0)
    slot = jnp.sum(earlier, axis=0, keepdims=True)
    place = (owner % nf) * nr + owner // nf
    keys[0:1, :] = jnp.where(slot == 0, place, -1)
    keys[1:2, :] = jnp.where(slot == 1, place, -1)

    def select(s):
        slot_id = lax.broadcasted_iota(jnp.int32, (mats, mats), 0)
        return jnp.where(slot_id == keys[s : s + 1, :], 1.0, 0.0).astype(BF)

    def gather(s):
        chosen = select(s)

        @pl.loop(0, half)
        def _(a):
            both = jnp.concatenate([g[a], g[a + half]], axis=0)
            out = mm(chosen, both, ((1,), (1,))).astype(BF)
            s_buf[s, :, a] = out.reshape(nf, nr, 128)

    def send_in(s):
        def regroup_two(k):
            first, second = lax.rem(fs + k, nf), lax.rem(fs + k + 1, nf)
            pair = jnp.concatenate(
                [s_buf[s, first].reshape(half * nr, 128), s_buf[s, second].reshape(half * nr, 128)], axis=1
            )
            out = mm(regroup[...], pair)
            t_buf[s, pl.ds(first * nr, nr)] = out[:, :128].reshape(nr, blk, 128).astype(BF)
            t_buf[s, pl.ds(second * nr, nr)] = out[:, 128:].reshape(nr, blk, 128).astype(BF)

        def send(to_r, to_f):
            pltpu.make_async_remote_copy(
                t_buf.at[s, to_f * nr + to_r], v_buf.at[s, rep * nf + fs], in_send.at[s], in_recv.at[s],
                device_id=(to_r, to_f), device_id_type=MESH,
            ).start()

        regroup_two(0)
        pltpu.make_async_copy(t_buf.at[s, fs * nr + rep], v_buf.at[s, rep * nf + fs], in_recv.at[s]).start()
        own_row(send)
        others(1, 2, send)

        @pl.loop(1, nf // 2)
        def _(k):
            regroup_two(2 * k)
            others(2 * k, 2 * k + 2, send)

    def send_out(s):
        def send(to_r, to_f):
            pltpu.make_async_remote_copy(
                w_buf.at[s, to_r * nf + to_f], u_buf.at[s, fs * nr + rep], out_send.at[s], out_recv.at[s],
                device_id=(to_r, to_f), device_id_type=MESH,
            ).start()

        pltpu.make_async_copy(w_buf.at[s, rep * nf + fs], u_buf.at[s, fs * nr + rep], out_recv.at[s]).start()
        own_row(send)
        others(1, nf, send)

    def assemble(s):
        @pl.loop(0, nr // 2)
        def _(q):
            pair = jnp.concatenate(
                [v_buf[s, pl.ds((2 * q + i) * nf, nf)].reshape(upper, 128) for i in range(2)], axis=1
            )
            out = mm(pair, swap[...]).astype(BF)
            cols = tile_cols(q, 128)
            zp[0:upper, cols] = out[:, :128]
            zp[upper : 2 * upper, cols] = out[:, 128:]

    def orthogonalize(s):
        wait_bytes(mom.at[s], mom_sem.at[s])
        own = rep * nf + fs
        mine = jnp.sum(jnp.where(owner_ref[...] == own, 1, 0), axis=1, keepdims=True)
        owned = mine > s

        def start(n, total):
            cols = tile_cols(n, 256)
            grad = mm(rows[0:hid, :], zp[:, cols])
            before = mom[s, :, cols]
            moment = (0.95 * before.astype(F32) + grad).astype(BF)
            new[s, :, cols] = jnp.where(owned, moment.astype(F32), before.astype(F32)).astype(BF)
            value = grad + 0.95 * moment.astype(F32)
            nest[:, cols] = value
            return total + jnp.sum(value * value, axis=0, keepdims=True)

        total = lax.fori_loop(0, width // 256, start, jnp.zeros((1, 256), F32))
        pltpu.make_async_copy(new.at[s], new_hbm.at[s], new_sem.at[s]).start()
        scale = 1.0 / (jnp.sqrt(jnp.sum(total, axis=1, keepdims=True)) + 1e-07)

        @pl.loop(0, width // 256)
        def _(n):
            cols = tile_cols(n, 256)
            x[0:hid, cols] = (nest[:, cols] * scale).astype(BF)

        if pad > hid:
            x[hid:pad, :] = jnp.zeros((pad - hid, width), BF)

        @pl.loop(0, ITERS)
        def _(turn):
            @pl.loop(0, pad // 256)
            def _(n):
                cols = tile_cols(n, 256)
                gram[:, cols] = mm(x[...], x[cols, :], ((1,), (1,))).astype(BF)

            @pl.loop(0, pad // 256)
            def _(n):
                cols = tile_cols(n, 256)
                part = gram[:, cols]
                square = mm(gram[...], part)
                mixed[:, cols] = (-4.775 * part.astype(F32) + 2.0315 * square).astype(BF)

            @pl.loop(0, width // 256)
            def _(n):
                cols = tile_cols(n, 256)
                part = x[:, cols]
                product = mm(mixed[...], part)
                x[:, cols] = (3.4445 * part.astype(F32) + product).astype(BF)

        factor = 0.2 * max(hid, width) ** 0.5

        @pl.loop(0, width // 256)
        def _(n):
            cols = tile_cols(n, 256)
            result = (factor * x[:, cols].astype(F32)).astype(BF)
            spread = mm(rows_t[...], result).astype(BF)
            for h in range(2):
                q = 2 * n + h
                both = jnp.concatenate(
                    [spread[0:upper, 128 * h : 128 * h + 128], spread[upper : 2 * upper, 128 * h : 128 * h + 128]],
                    axis=1,
                )
                out = mm(both, swap[...])
                w_buf[s, pl.ds(2 * q * nf, nf)] = out[:, :128].reshape(nf, blk, 128).astype(BF)
                w_buf[s, pl.ds((2 * q + 1) * nf, nf)] = out[:, 128:].reshape(nf, blk, 128).astype(BF)

    def ungroup(s):
        @pl.loop(0, nf // 2)
        def _(k):
            pair = jnp.concatenate(
                [u_buf[s, pl.ds((2 * k + i) * nr, nr)].reshape(nr * blk, 128) for i in range(2)], axis=1
            )
            out = mm(regroup_t[...], pair).astype(BF)
            s_buf[s, 2 * k] = out[:, :128].reshape(half, nr, 128)
            s_buf[s, 2 * k + 1] = out[:, 128:].reshape(half, nr, 128)

    loads[0].wait()
    gather(0)
    for load in loads[1:]:
        load.wait()
    pl.semaphore_wait(barrier, mats - 1)
    send_in(0)
    gather(1)
    send_in(1)

    for s in range(2):
        wait_bytes(v_buf.at[s], in_recv.at[s])
        assemble(s)
        orthogonalize(s)
        send_out(s)

    for s in range(2):
        wait_bytes(u_buf.at[s], out_recv.at[s])
        ungroup(s)
    chosen = [select(0), select(1)]

    @pl.loop(0, half)
    def _(a):
        out = sum(mm(s_buf[s, :, a].reshape(mats, 128), chosen[s], ((0,), (0,))) for s in range(2)).astype(BF)
        upd_ref[a] = out[0:64]
        upd_ref[a + half] = out[64:128]

    for s in range(2):
        wait_bytes(t_buf.at[s, pl.ds(0, mats - 1)], in_send.at[s])
        wait_bytes(w_buf.at[s, pl.ds(0, mats - 1)], out_send.at[s])
        wait_bytes(new.at[s], new_sem.at[s])


def one_hot(rows, cols, pairs):
    out = np.zeros((rows, cols), np.float32)
    for i, j in pairs:
        out[i, j] = 1.0
    return jnp.asarray(out, BF)


def on_device(grads, momentum, owner):
    nf, nr = lax.axis_size("fsdp"), lax.axis_size("rep")
    mats, tile_rows, tile_cols = grads.shape
    half = tile_rows // 2
    hid, width = nf * tile_rows, nr * tile_cols
    blk = half + 2
    upper = nf * blk
    pad = 2 * upper

    regroup_pairs = [(r * blk + a, a * nr + r) for r in range(nr) for a in range(half)]
    row_pairs = [
        (tile_rows * f + half * h + a, h * upper + f * blk + a)
        for f in range(nf) for h in range(2) for a in range(half)
    ]
    swap_pairs = [(i * 128 + j * 64 + c, j * 128 + i * 64 + c) for i in range(2) for j in range(2) for c in range(64)]
    flip = lambda pairs: [(j, i) for i, j in pairs]
    regroup = one_hot(nr * blk, half * nr, regroup_pairs)
    regroup_t = one_hot(half * nr, nr * blk, flip(regroup_pairs))
    rows = one_hot(pad, pad, row_pairs)
    rows_t = one_hot(pad, pad, flip(row_pairs))
    swap = one_hot(256, 256, swap_pairs)

    vmem = pl.BlockSpec(memory_space=pltpu.VMEM)
    hbm = pl.BlockSpec(memory_space=pl.ANY)
    cfg = (nr, nf, half, hid, width, pad)
    turned = grads.transpose(1, 2, 0)
    tables = [regroup, regroup_t, rows, rows_t, swap]
    by_f = pltpu.VMEM((2, nf, half, nr, 128), BF)
    tiles = pltpu.VMEM((2, mats, blk, 128), BF)
    update, new = pl.pallas_call(
        functools.partial(kernel, cfg),
        out_shape=(
            jax.ShapeDtypeStruct((tile_rows, tile_cols, mats), BF),
            jax.ShapeDtypeStruct(momentum.shape[1:], BF),
        ),
        in_specs=[vmem] + [hbm] * 7,
        out_specs=(vmem, hbm),
        scratch_shapes=[
            pltpu.VMEM(turned.shape, BF),
            *[pltpu.VMEM(table.shape, BF) for table in tables],
            pltpu.VMEM((2, mats), jnp.int32),
            by_f, tiles, tiles, tiles, tiles,
            pltpu.VMEM((2, hid, width), BF),
            pltpu.VMEM((2, hid, width), BF),
            pltpu.VMEM((pad, width), BF),
            pltpu.VMEM((hid, width), F32),
            pltpu.VMEM((pad, width), BF),
            pltpu.VMEM((pad, pad), BF),
            pltpu.VMEM((pad, pad), BF),
            pltpu.SemaphoreType.DMA((6,)),
            *[pltpu.SemaphoreType.DMA((2,)) for _ in range(6)],
        ],
        compiler_params=pltpu.CompilerParams(
            collective_id=0, has_side_effects=True, vmem_limit_bytes=58 * 1024 * 1024
        ),
        name="muon",
    )(owner[None, :], turned, momentum[0], *tables)
    return (update.transpose(2, 0, 1), new[None])


def solution(mesh):
    return jax.shard_map(
        on_device,
        mesh=mesh,
        in_specs=(P(None, "fsdp", "rep"), P(("rep", "fsdp"), None, None, None), P()),
        out_specs=(P(None, "fsdp", "rep"), P(("rep", "fsdp"), None, None, None)),
        check_vma=False,
    )
```

time: 487 us -> 170 us (0.35); the launches traced: 478 us -> 170 us
  local copies, waits for them, and re-layouts: 186 us -> 4.35 us
  Pallas kernels: 0 us -> 165 us
  waiting for transfers between devices: 124 us -> 0 us
  blocking collectives: 114 us -> 0 us
  other arithmetic: 18.4 us -> 0 us
  starting transfers between devices: 18.4 us -> 0 us
  matrix products: 13.5 us -> 0 us
    pallas_call x0 -> x1, Pallas kernels: none -> 165 us  [on_device(): pl.pallas_call(functools.partial(kernel, cfg), out_shape=(jax.ShapeDtypeS...]
    all_to_all x2 -> x0, waiting for transfers between devices: 124 us -> none  [the longest x1 63.6 us: on_device(): lax.all_to_all(lax.all_to_all(outgoing, 'rep', split_axis=3, concat_axis=...]
    all_to_all x2 -> x0, blocking collectives: 114 us -> none  [the longest x1 71.4 us: on_device(): lax.all_to_all(outgoing, 'rep', split_axis=3, concat_axis=3, tiled=True)]
    unnamed x16 -> x4, local copies, waits for them, and re-layouts: 114 us -> 4.35 us
    reshape x3 -> x0, local copies, waits for them, and re-layouts: 24 us -> none  [the longest x2 17.6 us: on_device(): result.reshape(capacity, fsdp_count, tile_rows, rep_count, tile_cols)]
    all_to_all x2 -> x0, starting transfers between devices: 18.4 us -> none  [the longest x1 10.9 us: on_device(): lax.all_to_all(lax.all_to_all(picked, 'rep', split_axis=3, concat_axis=3,...]
    transpose x3 -> x0, local copies, waits for them, and re-layouts: 17.9 us -> none  [the longest x2 11.6 us: on_device(): returned.transpose(3, 1, 0, 2, 4)]
    dot_general x4 -> x0, matrix products: 13.5 us -> none  [the longest x2 9.02 us: orthogonalize(): jnp.einsum('cik,ckj->cij', mixed, current, preferred_element_type=jnp.flo...]
  transfers between devices with their start and end apart: 2 -> 0, of which waited for: 2 -> 0; matrix products, arithmetic and copies ran while one was open for 1% -> 0% of each run, Pallas kernels for 0% -> 0%
where the time goes in v1:
time: 170 us
  Pallas kernels  165 us (97%)
  local copies, waits for them, and re-layouts  4.35 us (3%)
    pallas_call x1, Pallas kernels, on_device(): pl.pallas_call(functools.partial(kernel, cfg), out_shape=(jax.ShapeDtypeS...  165 us
    unnamed x4, local copies, waits for them, and re-layouts  4.35 us

profile of v1, /device:TPU:1, one launch (start us, length us, event | category | flops | bytes accessed | tf_op | source)
XLA Modules:
  0.0 170.4 jit_solution(18178067553900586222)
XLA Ops:
  0.6 165.4 %muon.1 = (bf16[44,64,256]{2,1,0:T(8,128)(2,1)}, bf16[2,704,1024]{2,1,0:T(8,128)(2,1)}) custom-call(s32[1,256]{1,0:T(1,128)} %bitcast.9, bf16[44,64,256]{2,1,0:T(8,128)(2,1)} %bitcast.8, bf16[2,704,1024]{2,1,0:T(8,128)(2,1)} %bitcast.5, bf16[384,352]{1,0:T(8,128)(2,1)} %constant.10.clone.regroup_hbm, bf16[352,384]{1,0:T(8,128)(2,1)} %constant.11.clone.regroup_t_hbm, ...), custom_call_target="tpu_custom_call" | custom-call | tf_op jit(solution)/shard_map/muon/pallas_call | solution.py:288
  166.0 0.0 copy-start
  166.0 2.8 %copy.12 = bf16[256,44,64]{0,2,1:T(8,128)(2,1)} copy(bf16[256,44,64]{0,2,1:T(8,128)(2,1)} %bitcast.7) | data formatting | bytes 2883584
  168.8 0.0 copy-done
  168.8 1.6 copy.13
Async XLA Ops:
  166.0 2.8 %copy-start = (bf16[2,704,1024]{2,1,0:T(8,128)(2,1)S(1)}, bf16[2,704,1024]{2,1,0:T(8,128)(2,1)}, u32[]{:S(2)}) copy-start(bf16[2,704,1024]{2,1,0:T(8,128)(2,1)} %get-tuple-element.5) | copy-start | bytes 8650756

commit v2 on v1

v2 whole, which is shorter than its diff:
```python
import functools

import jax
import jax.numpy as jnp
import numpy as np
from jax import lax
from jax.experimental import pallas as pl
from jax.experimental.pallas import tpu as pltpu
from jax.sharding import PartitionSpec as P

ITERS = 2
MESH = pl.DeviceIdType.MESH
BF = jnp.bfloat16
F32 = jnp.float32


def mm(a, b, dims=((1,), (0,))):
    return lax.dot_general(a, b, (dims, ((), ())), preferred_element_type=F32)


def wait_bytes(ref, sem):
    pltpu.make_async_copy(ref, ref, sem).wait()


def tile_cols(n, size):
    return pl.ds(pl.multiple_of(n * size, size), size)


def kernel(
    cfg, relayed,
    owner_ref, g_hbm, mom_hbm, regroup_hbm, regroup_t_hbm, rows_hbm, rows_t_hbm, swap_hbm,
    upd_ref, new_hbm,
    g, regroup, regroup_t, rows, rows_t, swap, keys,
    s_buf, t_buf, v_buf, w_buf, u_buf, mom, spun, new, nest, x, gram, mixed,
    load_sem, mom_sem, new_sem, in_send, in_recv, out_send, out_recv,
    *relay_refs,
):
    nr, nf, half, hid, width, pad = cfg
    rep, fs = lax.axis_index("rep"), lax.axis_index("fsdp")
    mats = nr * nf
    blk = half + 2
    upper = nf * blk
    nz = nf // 2
    z, core = fs // 2, lax.rem(fs, 2)
    lane = rep * nf + core * nz + z
    if relayed:
        (zs_buf, zr_buf, zt_buf, zv_buf, zu_buf, spread_in, spread_out,
         z_send, z_recv, p_send, zo_send, zo_recv, po_send, po_recv) = relay_refs

    loads = [(g_hbm, g), (regroup_hbm, regroup), (swap_hbm, swap), (rows_hbm, rows),
             (rows_t_hbm, rows_t), (regroup_t_hbm, regroup_t)]
    loads = [pltpu.make_async_copy(a, b, load_sem.at[i]) for i, (a, b) in enumerate(loads)]
    for load in loads:
        load.start()
    for s in range(2):
        pltpu.make_async_copy(mom_hbm.at[s], mom.at[s, pl.ds(0, hid)], mom_sem.at[s]).start()

    def others(first, last, visit):
        @pl.loop(first, last)
        def _(k):
            to_f = lax.rem(fs + k, nf)

            @pl.loop(0, nr, unroll=4)
            def _(j):
                visit(lax.rem(rep + j, nr), to_f)

    def own_row(visit):
        @pl.loop(1, nr)
        def _(j):
            visit(lax.rem(rep + j, nr), fs)

    barrier = pltpu.get_barrier_semaphore()

    def greet(to_r, to_f):
        pl.semaphore_signal(barrier, inc=1, device_id=(to_r, to_f), device_id_type=MESH)

    own_row(greet)
    others(1, nf, greet)

    owner = owner_ref[...]
    down = jnp.transpose(jnp.broadcast_to(owner, (mats, mats)))
    index = lax.broadcasted_iota(jnp.int32, (mats, mats), 0)
    order = lax.broadcasted_iota(jnp.int32, (mats, mats), 1)
    earlier = (down == owner) & (index < order)
    slot = jnp.sum(jnp.where(earlier, 1, 0), axis=0, keepdims=True)
    place = (owner % nf) * nr + owner // nf
    keys[0:1, :] = jnp.where(slot == 0, place, -1)
    if relayed:
        plane = jnp.where(slot == 1, (owner % nf) // 2, -1)
        plane_down = jnp.transpose(jnp.broadcast_to(plane, (mats, mats)))
        before = (plane_down == plane) & (index < order)
        rank = jnp.sum(jnp.where(before, 1, 0), axis=0, keepdims=True)
        keys[1:2, :] = jnp.where(slot == 1, plane * nr + rank, -1)
        member = (owner // nf) * 2 + owner % 2 + 1
        wide = half * nr
        column = lax.broadcasted_iota(jnp.int32, (wide, mats), 0) % nr
        here = jnp.where(keys[1:2, :] == z * nr + column, 1.0, 0.0).astype(BF)
        members = jnp.broadcast_to(member, (8, mats)).astype(F32).astype(BF)
        owner_of = mm(members, here, ((1,), (1,)))[0:1, :]
        line = lax.broadcasted_iota(jnp.int32, (2 * nr * blk, wide), 0)
        source = lax.broadcasted_iota(jnp.int32, (2 * nr * blk, wide), 1)
        wanted = (owner_of == (line // blk + 1).astype(F32)) & (line % blk == source // nr)
        wanted = jnp.where(wanted, 1.0, 0.0)
        spread_in[...] = wanted.astype(BF)
        spread_out[...] = jnp.transpose(wanted).astype(BF)
    else:
        keys[1:2, :] = jnp.where(slot == 1, place, -1)

    def select(s):
        places = nz * nr if relayed and s == 1 else mats
        slot_id = lax.broadcasted_iota(jnp.int32, (places, mats), 0)
        return jnp.where(slot_id == keys[s : s + 1, :], 1.0, 0.0).astype(BF)

    def gather(s):
        chosen = select(s)

        @pl.loop(0, half)
        def _(a):
            both = jnp.concatenate([g[a], g[a + half]], axis=0)
            out = mm(chosen, both, ((1,), (1,))).astype(BF)
            if relayed and s == 1:
                zs_buf[:, a] = out.reshape(nz, nr, 128)
            else:
                s_buf[s, :, a] = out.reshape(nf, nr, 128)

    def regroup_two(s, k):
        first, second = lax.rem(fs + k, nf), lax.rem(fs + k + 1, nf)
        pair = jnp.concatenate(
            [s_buf[s, first].reshape(half * nr, 128), s_buf[s, second].reshape(half * nr, 128)], axis=1
        )
        out = mm(regroup[...], pair)
        t_buf[s, pl.ds(first * nr, nr)] = out[:, :128].reshape(nr, blk, 128).astype(BF)
        t_buf[s, pl.ds(second * nr, nr)] = out[:, 128:].reshape(nr, blk, 128).astype(BF)

    def send_in(s, regrouped):
        def send(to_r, to_f):
            pltpu.make_async_remote_copy(
                t_buf.at[s, to_f * nr + to_r], v_buf.at[s, lane], in_send.at[s], in_recv.at[s],
                device_id=(to_r, to_f), device_id_type=MESH,
            ).start()

        if not regrouped:
            regroup_two(s, 0)
        pltpu.make_async_copy(t_buf.at[s, fs * nr + rep], v_buf.at[s, lane], in_recv.at[s]).start()
        own_row(send)
        others(1, 2, send)

        @pl.loop(1, nf // 2)
        def _(k):
            if not regrouped:
                regroup_two(s, 2 * k)
            others(2 * k, 2 * k + 2, send)

    def send_out(s):
        def send(to_r, to_f):
            pltpu.make_async_remote_copy(
                w_buf.at[s, to_r * nf + lax.rem(to_f, 2) * nz + to_f // 2], u_buf.at[s, fs * nr + rep], out_send.at[s], out_recv.at[s],
                device_id=(to_r, to_f), device_id_type=MESH,
            ).start()

        pltpu.make_async_copy(w_buf.at[s, lane], u_buf.at[s, fs * nr + rep], out_recv.at[s]).start()
        own_row(send)
        others(1, nf, send)

    def spin_momentum(s):
        wait_bytes(mom.at[s, pl.ds(0, hid)], mom_sem.at[s])
        if pad > hid:
            mom[s, hid:pad, :] = jnp.zeros((pad - hid, width), BF)

        @pl.loop(0, width // 256)
        def _(n):
            cols = tile_cols(n, 256)
            spun[s, :, cols] = mm(rows_t[...], mom[s, :, cols]).astype(BF)

    def store_momentum(s):
        own = rep * nf + fs
        mine = jnp.sum(jnp.where(owner_ref[...] == own, 1, 0), axis=1, keepdims=True)
        owned = mine > s

        @pl.loop(0, width // 256)
        def _(n):
            cols = tile_cols(n, 256)
            moment = mm(rows[0:hid, :], spun[s, :, cols])
            new[s, :, cols] = jnp.where(owned, moment, mom[s, 0:hid, cols].astype(F32)).astype(BF)

        pltpu.make_async_copy(new.at[s], new_hbm.at[s], new_sem.at[s]).start()

    def orthogonalize(s):
        def start(q, total):
            pair = jnp.concatenate(
                [v_buf[s, pl.ds((2 * q + i) * nf, nf)].reshape(upper, 128) for i in range(2)], axis=1
            )
            both = mm(pair, swap[...])
            cols = tile_cols(q, 128)
            for h in range(2):
                part = slice(h * upper, (h + 1) * upper)
                grad = both[:, 128 * h : 128 * h + 128]
                moment = (0.95 * spun[s, part, cols].astype(F32) + grad).astype(BF)
                spun[s, part, cols] = moment
                value = grad + 0.95 * moment.astype(F32)
                nest[part, cols] = value
                total = total + jnp.sum(value * value, axis=0, keepdims=True)
            return total

        total = lax.fori_loop(0, width // 128, start, jnp.zeros((1, 128), F32), unroll=2)
        scale = 1.0 / (jnp.sqrt(jnp.sum(total, axis=1, keepdims=True)) + 1e-07)

        @pl.loop(0, width // 256)
        def _(n):
            cols = tile_cols(n, 256)
            x[:, cols] = (nest[:, cols] * scale).astype(BF)

        @pl.loop(0, ITERS)
        def _(turn):
            for n in range(pad // 256):
                cols = slice(256 * n, 256 * n + 256)
                gram[:, cols] = mm(x[...], x[cols, :], ((1,), (1,))).astype(BF)

            for n in range(pad // 256):
                cols = slice(256 * n, 256 * n + 256)
                part = gram[:, cols]
                square = mm(gram[...], part)
                mixed[:, cols] = (-4.775 * part.astype(F32) + 2.0315 * square).astype(BF)

            for n in range(width // 256):
                cols = slice(256 * n, 256 * n + 256)
                part = x[:, cols]
                product = mm(mixed[...], part)
                x[:, cols] = (3.4445 * part.astype(F32) + product).astype(BF)

        factor = 0.2 * max(hid, width) ** 0.5

        @pl.loop(0, nr // 2, unroll=2)
        def _(q):
            cols = tile_cols(q, 128)
            both = jnp.concatenate(
                [(factor * x[h * upper : (h + 1) * upper, cols].astype(F32)).astype(BF) for h in range(2)], axis=1
            )
            out = mm(both, swap[...])
            for i in range(2):
                w_buf[s, pl.ds((2 * q + i) * nf, nf)] = (
                    out[:, 128 * i : 128 * i + 128].reshape(nf, blk, 128).astype(BF)
                )

    def ungroup(s):
        @pl.loop(0, nf // 2)
        def _(k):
            pair = jnp.concatenate(
                [u_buf[s, pl.ds((2 * k + i) * nr, nr)].reshape(nr * blk, 128) for i in range(2)], axis=1
            )
            out = mm(regroup_t[...], pair).astype(BF)
            s_buf[s, 2 * k] = out[:, :128].reshape(half, nr, 128)
            s_buf[s, 2 * k + 1] = out[:, 128:].reshape(half, nr, 128)

    def along_z(src, dst, send_sem, recv_sem):
        pltpu.make_async_copy(src.at[z], dst.at[z], recv_sem).start()

        @pl.loop(1, nz)
        def _(k):
            to_z = lax.rem(z + k, nz)
            pltpu.make_async_remote_copy(
                src.at[to_z], dst.at[z], send_sem, recv_sem,
                device_id=(rep, 2 * to_z + core), device_id_type=MESH,
            ).start()

    def in_plane(visit):
        @pl.loop(1, 2 * nr)
        def _(k):
            to = lax.rem(2 * rep + core + k, 2 * nr)
            visit(to, to // 2, 2 * z + lax.rem(to, 2))

    def relay_in():
        @pl.loop(0, nz // 2)
        def _(k):
            pair = jnp.concatenate([zr_buf[2 * k + i].reshape(half * nr, 128) for i in range(2)], axis=1)
            out = mm(spread_in[...], pair)
            for i in range(2):
                zt_buf[:, 2 * k + i] = out[:, 128 * i : 128 * i + 128].reshape(2 * nr, blk, 128).astype(BF)

        def send(to, to_r, to_f):
            pltpu.make_async_remote_copy(
                zt_buf.at[to], v_buf.at[1, pl.ds(rep * nf + core * nz, nz)], p_send, in_recv.at[1],
                device_id=(to_r, to_f), device_id_type=MESH,
            ).start()

        pltpu.make_async_copy(
            zt_buf.at[2 * rep + core], v_buf.at[1, pl.ds(rep * nf + core * nz, nz)], in_recv.at[1]
        ).start()
        in_plane(send)

    def plane_out():
        def send(to, to_r, to_f):
            pltpu.make_async_remote_copy(
                w_buf.at[1, pl.ds(to * nz, nz)], zv_buf.at[2 * rep + core], po_send, po_recv,
                device_id=(to_r, to_f), device_id_type=MESH,
            ).start()

        pltpu.make_async_copy(w_buf.at[1, pl.ds((2 * rep + core) * nz, nz)], zv_buf.at[2 * rep + core], po_recv).start()
        in_plane(send)

    def relay_out():
        @pl.loop(0, nz // 2)
        def _(k):
            pair = jnp.concatenate(
                [zv_buf[:, 2 * k + i].reshape(2 * nr * blk, 128) for i in range(2)], axis=1
            )
            out = mm(spread_out[...], pair).astype(BF)
            for i in range(2):
                zs_buf[2 * k + i] = out[:, 128 * i : 128 * i + 128].reshape(half, nr, 128)

    def unpack(second):
        chosen = [select(0), select(1)]

        @pl.loop(0, half)
        def _(a):
            first = mm(s_buf[0, :, a].reshape(mats, 128), chosen[0], ((0,), (0,)))
            out = (first + mm(second(a), chosen[1], ((0,), (0,)))).astype(BF)
            upd_ref[a] = out[0:64]
            upd_ref[a + half] = out[64:128]

    def all_but_one(ref):
        return ref.at[pl.ds(0, ref.shape[0] - 1)]

    loads[0].wait()
    if relayed:
        gather(1)
        pl.semaphore_wait(barrier, mats - 1)
        along_z(zs_buf, zr_buf, z_send, z_recv)
        gather(0)
        for load in loads[1:]:
            load.wait()

        @pl.loop(0, nf // 2)
        def _(k):
            regroup_two(0, 2 * k)

        spin_momentum(1)
        spin_momentum(0)

        wait_bytes(zr_buf, z_recv)
        relay_in()
        send_in(0, True)
        wait_bytes(v_buf.at[1], in_recv.at[1])
        orthogonalize(1)
        plane_out()

        wait_bytes(v_buf.at[0], in_recv.at[0])
        orthogonalize(0)
        send_out(0)

        wait_bytes(zv_buf, po_recv)
        wait_bytes(all_but_one(zs_buf), z_send)
        relay_out()
        along_z(zs_buf, zu_buf, zo_send, zo_recv)
        store_momentum(1)
        store_momentum(0)

        wait_bytes(u_buf.at[0], out_recv.at[0])
        ungroup(0)
        wait_bytes(zu_buf, zo_recv)
        unpack(lambda a: zu_buf[:, a].reshape(nz * nr, 128))
        wait_bytes(all_but_one(zt_buf), p_send)
        wait_bytes(all_but_one(zv_buf), po_send)
        wait_bytes(all_but_one(zs_buf), zo_send)
    else:
        gather(0)
        for load in loads[1:]:
            load.wait()
        pl.semaphore_wait(barrier, mats - 1)
        send_in(0, False)
        gather(1)
        send_in(1, False)
        spin_momentum(0)
        spin_momentum(1)
        for s in range(2):
            wait_bytes(v_buf.at[s], in_recv.at[s])
            orthogonalize(s)
            send_out(s)
        for s in range(2):
            store_momentum(s)
        for s in range(2):
            wait_bytes(u_buf.at[s], out_recv.at[s])
            ungroup(s)
        unpack(lambda a: s_buf[1, :, a].reshape(mats, 128))

    for s in range(2):
        wait_bytes(new.at[s], new_sem.at[s])
    for s in range(1 if relayed else 2):
        wait_bytes(all_but_one(t_buf.at[s]), in_send.at[s])
        wait_bytes(all_but_one(w_buf.at[s]), out_send.at[s])


def one_hot(rows, cols, pairs):
    out = np.zeros((rows, cols), np.float32)
    for i, j in pairs:
        out[i, j] = 1.0
    return jnp.asarray(out, BF)


def on_device(grads, momentum, owner):
    nf, nr = lax.axis_size("fsdp"), lax.axis_size("rep")
    mats, tile_rows, tile_cols = grads.shape
    half = tile_rows // 2
    hid, width = nf * tile_rows, nr * tile_cols
    blk = half + 2
    upper = nf * blk
    pad = 2 * upper
    nz = nf // 2

    regroup_pairs = [(r * blk + a, a * nr + r) for r in range(nr) for a in range(half)]
    row_pairs = [
        (tile_rows * f + half * h + a, h * upper + (f % 2 * nz + f // 2) * blk + a)
        for f in range(nf) for h in range(2) for a in range(half)
    ]
    swap_pairs = [(i * 128 + j * 64 + c, j * 128 + i * 64 + c) for i in range(2) for j in range(2) for c in range(64)]
    flip = lambda pairs: [(j, i) for i, j in pairs]
    regroup = one_hot(nr * blk, half * nr, regroup_pairs)
    regroup_t = one_hot(half * nr, nr * blk, flip(regroup_pairs))
    rows = one_hot(pad, pad, row_pairs)
    rows_t = one_hot(pad, pad, flip(row_pairs))
    swap = one_hot(256, 256, swap_pairs)

    vmem = pl.BlockSpec(memory_space=pltpu.VMEM)
    hbm = pl.BlockSpec(memory_space=pl.ANY)
    cfg = (nr, nf, half, hid, width, pad)
    turned = grads.transpose(1, 2, 0)
    tables = [regroup, regroup_t, rows, rows_t, swap]
    by_f = pltpu.VMEM((2, nf, half, nr, 128), BF)
    tiles = pltpu.VMEM((2, mats, blk, 128), BF)
    by_z = pltpu.VMEM((nz, half, nr, 128), BF)
    in_plane = pltpu.VMEM((2 * nr, nz, blk, 128), BF)
    one = pltpu.SemaphoreType.DMA(())
    relay_scratch = [
        by_z, by_z, in_plane, in_plane, by_z,
        pltpu.VMEM((2 * nr * blk, half * nr), BF),
        pltpu.VMEM((half * nr, 2 * nr * blk), BF),
        *[one for _ in range(7)],
    ]

    def run(relayed, operands):
        return pl.pallas_call(
            functools.partial(kernel, cfg, relayed),
            out_shape=(
                jax.ShapeDtypeStruct((tile_rows, tile_cols, mats), BF),
                jax.ShapeDtypeStruct(momentum.shape[1:], BF),
            ),
            in_specs=[vmem] + [hbm] * 7,
            out_specs=(vmem, hbm),
            scratch_shapes=[
                pltpu.VMEM(turned.shape, BF),
                *[pltpu.VMEM(table.shape, BF) for table in tables],
                pltpu.VMEM((2, mats), jnp.int32),
                by_f, tiles, tiles, tiles, tiles,
                pltpu.VMEM((2, pad, width), BF),
                pltpu.VMEM((2, pad, width), BF),
                pltpu.VMEM((2, hid, width), BF),
                pltpu.VMEM((pad, width), F32),
                pltpu.VMEM((pad, width), BF),
                pltpu.VMEM((pad, pad), BF),
                pltpu.VMEM((pad, pad), BF),
                pltpu.SemaphoreType.DMA((6,)),
                *[pltpu.SemaphoreType.DMA((2,)) for _ in range(6)],
                *(relay_scratch if relayed else []),
            ],
            compiler_params=pltpu.CompilerParams(
                collective_id=1 if relayed else 0, has_side_effects=True, vmem_limit_bytes=58 * 1024 * 1024
            ),
            name="muon_relayed" if relayed else "muon_direct",
        )(*operands)

    order = jnp.arange(mats, dtype=jnp.int32)
    second = (owner[:, None] == owner[None, :]) & (order[:, None] < order[None, :])
    plane = (owner % nf) // 2
    in_each = second[None] & (plane[None, None, :] == jnp.arange(nz, dtype=jnp.int32)[:, None, None])
    fits = jnp.max(jnp.sum(in_each.astype(jnp.int32), axis=(1, 2))) <= nr
    operands = (owner[None, :], turned, momentum[0], *tables)
    update, new = lax.cond(fits, functools.partial(run, True), functools.partial(run, False), operands)
    return (update.transpose(2, 0, 1), new[None])


def solution(mesh):
    return jax.shard_map(
        on_device,
        mesh=mesh,
        in_specs=(P(None, "fsdp", "rep"), P(("rep", "fsdp"), None, None, None), P()),
        out_specs=(P(None, "fsdp", "rep"), P(("rep", "fsdp"), None, None, None)),
        check_vma=False,
    )
```

time: 170 us -> 162 us (0.953)
  the two profiles are of different devices: /device:TPU:1 before, /device:TPU:93 now
where the time goes in v2:
time: 162 us
  Pallas kernels  156 us (96%)
  local copies, waits for them, and re-layouts  2.68 us (2%)
  other arithmetic  2.54 us (2%)
    pallas_call x1, Pallas kernels, run(): pl.pallas_call(functools.partial(kernel, cfg, relayed), out_shape=(jax.Sh...  156 us

profile of v2, /device:TPU:93, one launch (start us, length us, event | category | flops | bytes accessed | tf_op | source)
XLA Modules:
  0.0 162.3 jit_solution(11973264724443282165)
XLA Ops:
  0.6 0.7 and_select_fusion
  1.3 0.9 fusion
  2.2 0.3 convert_reduce_fusion
  2.5 0.6 reduce_max.9
  3.8 155.8 %conditional.1 = (bf16[44,64,256]{2,1,0:T(8,128)(2,1)S(1)}, bf16[1,2,704,1024]{3,2,1,0:T(8,128)(2,1)S(1)}) conditional(s32[]{:T(128)} %convert_element_type.7, (s32[256]{0:T(256)}, bf16[1,2,704,1024]{3,2,1,0:T(8,128)(2,1)}, bf16[44,64,256]{2,1,0:T(8,128)(2,1)}, bf16[384,352]{1,0:T(8,128)(2,1)}, bf16[352,384]{1,0:T(8,128)(2,1)}, ...), branch_computations={%region_2.3_spmd, %region_3.4_spmd} | conditional | bytes 16 | solution.py:477
  4.0 155.6 %muon_relayed.1 = (bf16[44,64,256]{2,1,0:T(8,128)(2,1)S(1)}, bf16[2,704,1024]{2,1,0:T(8,128)(2,1)S(1)}) custom-call(s32[1,256]{1,0:T(1,128)} %bitcast.16, bf16[44,64,256]{2,1,0:T(8,128)(2,1)} %get-tuple-element.52.g_hbm, bf16[2,704,1024]{2,1,0:T(8,128)(2,1)} %bitcast.9, bf16[384,352]{1,0:T(8,128)(2,1)} %get-tuple-element.54.regroup_hbm, ...), custom_call_target="tpu_custom_call" | custom-call | tf_op jit(solution)/shard_map/cond/branch_1_fun/muon_relayed/pallas_call | solution.py:441
  159.6 1.1 copy.16
  160.7 1.6 copy.17
  (1 shorter events, 0.0 us)

commit v3 on v2

--- a/solution.py
+++ b/solution.py
@@ -55,27 +55,42 @@
     for s in range(2):
         pltpu.make_async_copy(mom_hbm.at[s], mom.at[s, pl.ds(0, hid)], mom_sem.at[s]).start()
 
-    def others(first, last, visit):
-        @pl.loop(first, last)
+    side = 4
+    rx, ry = rep // side, lax.rem(rep, side)
+
+    def moved(j):
+        return lax.rem(rx + j, side) * side + lax.rem(ry + j // side + j, side)
+
+    def faces(dz, dc):
+        return 2 * lax.rem(z + dz, nz) + lax.rem(core + dc, 2)
+
+    def everyone(visit):
+        @pl.loop(0, nz // 2 - 1)
         def _(k):
-            to_f = lax.rem(fs + k, nf)
-
-            @pl.loop(0, nr, unroll=4)
+            @pl.loop(0, nr)
             def _(j):
-                visit(lax.rem(rep + j, nr), to_f)
-
-    def own_row(visit):
+                to_r = moved(j)
+                for dc in range(2):
+                    visit(to_r, faces(k + 1, dc))
+                    visit(to_r, faces(nz - 1 - k, dc))
+
+        for dc in range(2):
+            visit(rep, faces(nz // 2, dc))
+        visit(rep, faces(0, 1))
+
         @pl.loop(1, nr)
         def _(j):
-            visit(lax.rem(rep + j, nr), fs)
+            to_r = moved(j)
+            for dc in range(2):
+                visit(to_r, faces(nz // 2, dc))
+                visit(to_r, faces(0, dc))
 
     barrier = pltpu.get_barrier_semaphore()
 
     def greet(to_r, to_f):
         pl.semaphore_signal(barrier, inc=1, device_id=(to_r, to_f), device_id_type=MESH)
 
-    own_row(greet)
-    others(1, nf, greet)
+    everyone(greet)
 
     owner = owner_ref[...]
     down = jnp.transpose(jnp.broadcast_to(owner, (mats, mats)))
@@ -124,7 +139,7 @@
                 s_buf[s, :, a] = out.reshape(nf, nr, 128)
 
     def regroup_two(s, k):
-        first, second = lax.rem(fs + k, nf), lax.rem(fs + k + 1, nf)
+        first, second = k, k + 1
         pair = jnp.concatenate(
             [s_buf[s, first].reshape(half * nr, 128), s_buf[s, second].reshape(half * nr, 128)], axis=1
         )
@@ -132,6 +147,11 @@
         t_buf[s, pl.ds(first * nr, nr)] = out[:, :128].reshape(nr, blk, 128).astype(BF)
         t_buf[s, pl.ds(second * nr, nr)] = out[:, 128:].reshape(nr, blk, 128).astype(BF)
 
+    def regroup_all(s):
+        @pl.loop(0, nf // 2)
+        def _(k):
+            regroup_two(s, 2 * k)
+
     def send_in(s, regrouped):
         def send(to_r, to_f):
             pltpu.make_async_remote_copy(
@@ -140,16 +160,9 @@
             ).start()
 
         if not regrouped:
-            regroup_two(s, 0)
+            regroup_all(s)
         pltpu.make_async_copy(t_buf.at[s, fs * nr + rep], v_buf.at[s, lane], in_recv.at[s]).start()
-        own_row(send)
-        others(1, 2, send)
-
-        @pl.loop(1, nf // 2)
-        def _(k):
-            if not regrouped:
-                regroup_two(s, 2 * k)
-            others(2 * k, 2 * k + 2, send)
+        everyone(send)
 
     def send_out(s):
         def send(to_r, to_f):
@@ -159,8 +172,7 @@
             ).start()
 
         pltpu.make_async_copy(w_buf.at[s, lane], u_buf.at[s, fs * nr + rep], out_recv.at[s]).start()
-        own_row(send)
-        others(1, nf, send)
+        everyone(send)
 
     def spin_momentum(s):
         wait_bytes(mom.at[s, pl.ds(0, hid)], mom_sem.at[s])
@@ -255,19 +267,27 @@
     def along_z(src, dst, send_sem, recv_sem):
         pltpu.make_async_copy(src.at[z], dst.at[z], recv_sem).start()
 
-        @pl.loop(1, nz)
-        def _(k):
-            to_z = lax.rem(z + k, nz)
+        def send(dz):
+            to_z = lax.rem(z + dz, nz)
             pltpu.make_async_remote_copy(
                 src.at[to_z], dst.at[z], send_sem, recv_sem,
                 device_id=(rep, 2 * to_z + core), device_id_type=MESH,
             ).start()
 
+        send(nz // 2)
+        for k in range(nz // 2 - 1, 0, -1):
+            send(k)
+            send(nz - k)
+
     def in_plane(visit):
-        @pl.loop(1, 2 * nr)
-        def _(k):
-            to = lax.rem(2 * rep + core + k, 2 * nr)
-            visit(to, to // 2, 2 * z + lax.rem(to, 2))
+        visit(2 * rep + 1 - core, rep, 2 * z + 1 - core)
+
+        @pl.loop(1, nr)
+        def _(j):
+            to_r = moved(j)
+            for dc in range(2):
+                to_c = lax.rem(core + dc, 2)
+                visit(2 * to_r + to_c, to_r, 2 * z + to_c)
 
     def relay_in():
         @pl.loop(0, nz // 2)
@@ -329,11 +349,7 @@
         gather(0)
         for load in loads[1:]:
             load.wait()
-
-        @pl.loop(0, nf // 2)
-        def _(k):
-            regroup_two(0, 2 * k)
-
+        regroup_all(0)
         spin_momentum(1)
         spin_momentum(0)
 

time: 162 us -> 157 us (0.969)
  the two profiles are of different devices: /device:TPU:93 before, /device:TPU:1 now
where the time goes in v3:
time: 157 us
  Pallas kernels  150 us (96%)
  local copies, waits for them, and re-layouts  2.68 us (2%)
  other arithmetic  2.54 us (2%)
    pallas_call x1, Pallas kernels, run(): pl.pallas_call(functools.partial(kernel, cfg, relayed), out_shape=(jax.Sh...  150 us

profile of v3, /device:TPU:1, one launch (start us, length us, event | category | flops | bytes accessed | tf_op | source)
XLA Modules:
  0.0 157.1 jit_solution(15144445464352223083)
XLA Ops:
  0.6 0.7 and_select_fusion
  1.3 0.9 fusion
  2.2 0.3 convert_reduce_fusion
  2.5 0.6 reduce_max.9
  3.8 150.5 %conditional.1 = (bf16[44,64,256]{2,1,0:T(8,128)(2,1)S(1)}, bf16[1,2,704,1024]{3,2,1,0:T(8,128)(2,1)S(1)}) conditional(s32[]{:T(128)} %convert_element_type.7, (s32[256]{0:T(256)}, bf16[1,2,704,1024]{3,2,1,0:T(8,128)(2,1)}, bf16[44,64,256]{2,1,0:T(8,128)(2,1)}, bf16[384,352]{1,0:T(8,128)(2,1)}, bf16[352,384]{1,0:T(8,128)(2,1)}, ...), branch_computations={%region_2.3_spmd, %region_3.4_spmd} | conditional | bytes 16 | solution.py:493
  4.0 150.3 %muon_relayed.1 = (bf16[44,64,256]{2,1,0:T(8,128)(2,1)S(1)}, bf16[2,704,1024]{2,1,0:T(8,128)(2,1)S(1)}) custom-call(s32[1,256]{1,0:T(1,128)} %bitcast.16, bf16[44,64,256]{2,1,0:T(8,128)(2,1)} %get-tuple-element.52.g_hbm, bf16[2,704,1024]{2,1,0:T(8,128)(2,1)} %bitcast.9, bf16[384,352]{1,0:T(8,128)(2,1)} %get-tuple-element.54.regroup_hbm, ...), custom_call_target="tpu_custom_call" | custom-call | tf_op jit(solution)/shard_map/cond/branch_1_fun/muon_relayed/pallas_call | solution.py:457
  154.4 1.1 copy.16
  155.5 1.6 %copy.17 = bf16[1,2,704,1024]{3,2,1,0:T(8,128)(2,1)} copy(bf16[1,2,704,1024]{3,2,1,0:T(8,128)(2,1)S(1)} %get-tuple-element.74) | data formatting | bytes 5767168
  (1 shorter events, 0.0 us)

commit v4 on v3

--- a/solution.py
+++ b/solution.py
@@ -87,10 +87,10 @@
 
     barrier = pltpu.get_barrier_semaphore()
 
-    def greet(to_r, to_f):
+    def greet(t):
+        to_r = lax.rem(rx + t, side) * side + lax.rem(ry + t // side, side)
+        to_f = lax.rem(fs + t // nr, nf)
         pl.semaphore_signal(barrier, inc=1, device_id=(to_r, to_f), device_id_type=MESH)
-
-    everyone(greet)
 
     owner = owner_ref[...]
     down = jnp.transpose(jnp.broadcast_to(owner, (mats, mats)))
@@ -106,6 +106,10 @@
         before = (plane_down == plane) & (index < order)
         rank = jnp.sum(jnp.where(before, 1, 0), axis=0, keepdims=True)
         keys[1:2, :] = jnp.where(slot == 1, plane * nr + rank, -1)
+    else:
+        keys[1:2, :] = jnp.where(slot == 1, place, -1)
+
+    def relay_matrices():
         member = (owner // nf) * 2 + owner % 2 + 1
         wide = half * nr
         column = lax.broadcasted_iota(jnp.int32, (wide, mats), 0) % nr
@@ -118,25 +122,34 @@
         wanted = jnp.where(wanted, 1.0, 0.0)
         spread_in[...] = wanted.astype(BF)
         spread_out[...] = jnp.transpose(wanted).astype(BF)
-    else:
-        keys[1:2, :] = jnp.where(slot == 1, place, -1)
 
     def select(s):
         places = nz * nr if relayed and s == 1 else mats
         slot_id = lax.broadcasted_iota(jnp.int32, (places, mats), 0)
         return jnp.where(slot_id == keys[s : s + 1, :], 1.0, 0.0).astype(BF)
 
-    def gather(s):
+    def gather(s, greeting):
         chosen = select(s)
-
-        @pl.loop(0, half)
-        def _(a):
+        def one_row(a):
             both = jnp.concatenate([g[a], g[a + half]], axis=0)
             out = mm(chosen, both, ((1,), (1,))).astype(BF)
             if relayed and s == 1:
                 zs_buf[:, a] = out.reshape(nz, nr, 128)
             else:
                 s_buf[s, :, a] = out.reshape(nf, nr, 128)
+
+        rounds = (mats - 1) // 15
+
+        @pl.loop(0, rounds)
+        def _(a):
+            if greeting:
+                for t in range(15):
+                    greet(15 * a + t + 1)
+            one_row(a)
+
+        @pl.loop(rounds, half)
+        def _(a):
+            one_row(a)
 
     def regroup_two(s, k):
         first, second = k, k + 1
@@ -167,11 +180,11 @@
     def send_out(s):
         def send(to_r, to_f):
             pltpu.make_async_remote_copy(
-                w_buf.at[s, to_r * nf + lax.rem(to_f, 2) * nz + to_f // 2], u_buf.at[s, fs * nr + rep], out_send.at[s], out_recv.at[s],
+                w_buf.at[s, to_r * nf + lax.rem(to_f, 2) * nz + to_f // 2], u_buf.at[s, fs * nr + rep], out_send.at[s], out_recv.at[s, z],
                 device_id=(to_r, to_f), device_id_type=MESH,
             ).start()
 
-        pltpu.make_async_copy(w_buf.at[s, lane], u_buf.at[s, fs * nr + rep], out_recv.at[s]).start()
+        pltpu.make_async_copy(w_buf.at[s, lane], u_buf.at[s, fs * nr + rep], out_recv.at[s, z]).start()
         everyone(send)
 
     def spin_momentum(s):
@@ -197,7 +210,7 @@
 
         pltpu.make_async_copy(new.at[s], new_hbm.at[s], new_sem.at[s]).start()
 
-    def orthogonalize(s):
+    def orthogonalize(s, before_last):
         def start(q, total):
             pair = jnp.concatenate(
                 [v_buf[s, pl.ds((2 * q + i) * nf, nf)].reshape(upper, 128) for i in range(2)], axis=1
@@ -214,7 +227,7 @@
                 total = total + jnp.sum(value * value, axis=0, keepdims=True)
             return total
 
-        total = lax.fori_loop(0, width // 128, start, jnp.zeros((1, 128), F32), unroll=2)
+        total = lax.fori_loop(0, width // 128, start, jnp.zeros((1, 128), F32))
         scale = 1.0 / (jnp.sqrt(jnp.sum(total, axis=1, keepdims=True)) + 1e-07)
 
         @pl.loop(0, width // 256)
@@ -222,27 +235,35 @@
             cols = tile_cols(n, 256)
             x[:, cols] = (nest[:, cols] * scale).astype(BF)
 
-        @pl.loop(0, ITERS)
-        def _(turn):
-            for n in range(pad // 256):
-                cols = slice(256 * n, 256 * n + 256)
+        def mix():
+            @pl.loop(0, pad // 256)
+            def _(n):
+                cols = tile_cols(n, 256)
                 gram[:, cols] = mm(x[...], x[cols, :], ((1,), (1,))).astype(BF)
 
-            for n in range(pad // 256):
-                cols = slice(256 * n, 256 * n + 256)
+            @pl.loop(0, pad // 256)
+            def _(n):
+                cols = tile_cols(n, 256)
                 part = gram[:, cols]
                 square = mm(gram[...], part)
                 mixed[:, cols] = (-4.775 * part.astype(F32) + 2.0315 * square).astype(BF)
 
-            for n in range(width // 256):
-                cols = slice(256 * n, 256 * n + 256)
+        def product():
+            @pl.loop(0, width // 256)
+            def _(n):
+                cols = tile_cols(n, 256)
                 part = x[:, cols]
-                product = mm(mixed[...], part)
-                x[:, cols] = (3.4445 * part.astype(F32) + product).astype(BF)
-
+                x[:, cols] = (3.4445 * part.astype(F32) + mm(mixed[...], part)).astype(BF)
+
+        for _ in range(ITERS - 1):
+            mix()
+            product()
+        mix()
+        before_last()
+        product()
         factor = 0.2 * max(hid, width) ** 0.5
 
-        @pl.loop(0, nr // 2, unroll=2)
+        @pl.loop(0, nr // 2)
         def _(q):
             cols = tile_cols(q, 128)
             both = jnp.concatenate(
@@ -255,14 +276,24 @@
                 )
 
     def ungroup(s):
-        @pl.loop(0, nf // 2)
-        def _(k):
+        def one(dz):
+            k = lax.rem(z + dz, nz)
+            wait_bytes(u_buf.at[s, pl.ds(2 * k * nr, 2 * nr)], out_recv.at[s, k])
             pair = jnp.concatenate(
                 [u_buf[s, pl.ds((2 * k + i) * nr, nr)].reshape(nr * blk, 128) for i in range(2)], axis=1
             )
             out = mm(regroup_t[...], pair).astype(BF)
             s_buf[s, 2 * k] = out[:, :128].reshape(half, nr, 128)
             s_buf[s, 2 * k + 1] = out[:, 128:].reshape(half, nr, 128)
+
+        @pl.loop(0, nz // 2 - 1)
+        def _(k):
+            one(k + 1)
+            one(nz - 1 - k)
+
+        @pl.loop(0, 2)
+        def _(k):
+            one(k * (nz // 2))
 
     def along_z(src, dst, send_sem, recv_sem):
         pltpu.make_async_copy(src.at[z], dst.at[z], recv_sem).start()
@@ -328,13 +359,23 @@
             for i in range(2):
                 zs_buf[2 * k + i] = out[:, 128 * i : 128 * i + 128].reshape(half, nr, 128)
 
-    def unpack(second):
-        chosen = [select(0), select(1)]
+    def block(a):
+        return pl.ds(pl.multiple_of(lax.rem(a, 6) * 128, 128), 128), tile_cols(a // 6, 256)
+
+    def unpack_second(tile):
+        chosen = select(1)
 
         @pl.loop(0, half)
         def _(a):
-            first = mm(s_buf[0, :, a].reshape(mats, 128), chosen[0], ((0,), (0,)))
-            out = (first + mm(second(a), chosen[1], ((0,), (0,)))).astype(BF)
+            nest[block(a)] = mm(tile(a), chosen, ((0,), (0,)))
+
+    def unpack():
+        chosen = select(0)
+
+        @pl.loop(0, half)
+        def _(a):
+            first = mm(s_buf[0, :, a].reshape(mats, 128), chosen, ((0,), (0,)))
+            out = (first + nest[block(a)]).astype(BF)
             upd_ref[a] = out[0:64]
             upd_ref[a + half] = out[64:128]
 
@@ -343,10 +384,11 @@
 
     loads[0].wait()
     if relayed:
-        gather(1)
+        gather(1, True)
         pl.semaphore_wait(barrier, mats - 1)
         along_z(zs_buf, zr_buf, z_send, z_recv)
-        gather(0)
+        gather(0, False)
+        relay_matrices()
         for load in loads[1:]:
             load.wait()
         regroup_all(0)
@@ -357,47 +399,47 @@
         relay_in()
         send_in(0, True)
         wait_bytes(v_buf.at[1], in_recv.at[1])
-        orthogonalize(1)
+        orthogonalize(1, lambda: None)
         plane_out()
 
         wait_bytes(v_buf.at[0], in_recv.at[0])
-        orthogonalize(0)
+        def second_back():
+            wait_bytes(zv_buf, po_recv)
+            wait_bytes(all_but_one(zs_buf), z_send)
+            relay_out()
+            along_z(zs_buf, zu_buf, zo_send, zo_recv)
+
+        orthogonalize(0, second_back)
         send_out(0)
-
-        wait_bytes(zv_buf, po_recv)
-        wait_bytes(all_but_one(zs_buf), z_send)
-        relay_out()
-        along_z(zs_buf, zu_buf, zo_send, zo_recv)
         store_momentum(1)
         store_momentum(0)
-
-        wait_bytes(u_buf.at[0], out_recv.at[0])
+        wait_bytes(zu_buf, zo_recv)
+        unpack_second(lambda a: zu_buf[:, a].reshape(nz * nr, 128))
         ungroup(0)
-        wait_bytes(zu_buf, zo_recv)
-        unpack(lambda a: zu_buf[:, a].reshape(nz * nr, 128))
+        unpack()
         wait_bytes(all_but_one(zt_buf), p_send)
         wait_bytes(all_but_one(zv_buf), po_send)
         wait_bytes(all_but_one(zs_buf), zo_send)
     else:
-        gather(0)
+        gather(0, True)
         for load in loads[1:]:
             load.wait()
         pl.semaphore_wait(barrier, mats - 1)
         send_in(0, False)
-        gather(1)
+        gather(1, False)
         send_in(1, False)
         spin_momentum(0)
         spin_momentum(1)
         for s in range(2):
             wait_bytes(v_buf.at[s], in_recv.at[s])
-            orthogonalize(s)
+            orthogonalize(s, lambda: None)
             send_out(s)
         for s in range(2):
             store_momentum(s)
-        for s in range(2):
-            wait_bytes(u_buf.at[s], out_recv.at[s])
-            ungroup(s)
-        unpack(lambda a: s_buf[1, :, a].reshape(mats, 128))
+        ungroup(1)
+        unpack_second(lambda a: s_buf[1, :, a].reshape(mats, 128))
+        ungroup(0)
+        unpack()
 
     for s in range(2):
         wait_bytes(new.at[s], new_sem.at[s])
@@ -475,7 +517,8 @@
                 pltpu.VMEM((pad, pad), BF),
                 pltpu.VMEM((pad, pad), BF),
                 pltpu.SemaphoreType.DMA((6,)),
-                *[pltpu.SemaphoreType.DMA((2,)) for _ in range(6)],
+                *[pltpu.SemaphoreType.DMA((2,)) for _ in range(5)],
+                pltpu.SemaphoreType.DMA((2, nz)),
                 *(relay_scratch if relayed else []),
             ],
             compiler_params=pltpu.CompilerParams(

time: 157 us -> 180 us (1.15)
  Pallas kernels: 150 us -> 173 us
    pallas_call x1, Pallas kernels: 150 us -> 173 us  [run(): pl.pallas_call(functools.partial(kernel, cfg, relayed), out_shape=(jax.Sh...]
where the time goes in v4:
time: 180 us
  Pallas kernels  173 us (96%)
  local copies, waits for them, and re-layouts  2.68 us (1%)
  other arithmetic  2.54 us (1%)
    pallas_call x1, Pallas kernels, run(): pl.pallas_call(functools.partial(kernel, cfg, relayed), out_shape=(jax.Sh...  173 us

profile of v4, /device:TPU:1, one launch (start us, length us, event | category | flops | bytes accessed | tf_op | source)
XLA Modules:
  0.0 180.1 jit_solution(8728586649320184974)
XLA Ops:
  0.6 0.7 and_select_fusion
  1.3 0.9 fusion
  2.2 0.3 convert_reduce_fusion
  2.5 0.6 reduce_max.9
  3.8 173.6 %conditional.1 = (bf16[44,64,256]{2,1,0:T(8,128)(2,1)S(1)}, bf16[1,2,704,1024]{3,2,1,0:T(8,128)(2,1)S(1)}) conditional(s32[]{:T(128)} %convert_element_type.7, (s32[256]{0:T(256)}, bf16[1,2,704,1024]{3,2,1,0:T(8,128)(2,1)}, bf16[44,64,256]{2,1,0:T(8,128)(2,1)}, bf16[384,352]{1,0:T(8,128)(2,1)}, bf16[352,384]{1,0:T(8,128)(2,1)}, ...), branch_computations={%region_2.3_spmd, %region_3.4_spmd} | conditional | bytes 16 | solution.py:536
  4.0 173.4 %muon_relayed.1 = (bf16[44,64,256]{2,1,0:T(8,128)(2,1)S(1)}, bf16[2,704,1024]{2,1,0:T(8,128)(2,1)S(1)}) custom-call(s32[1,256]{1,0:T(1,128)} %bitcast.16, bf16[44,64,256]{2,1,0:T(8,128)(2,1)} %get-tuple-element.52.g_hbm, bf16[2,704,1024]{2,1,0:T(8,128)(2,1)} %bitcast.9, bf16[384,352]{1,0:T(8,128)(2,1)} %get-tuple-element.54.regroup_hbm, ...), custom_call_target="tpu_custom_call" | custom-call | tf_op jit(solution)/shard_map/cond/branch_1_fun/muon_relayed/pallas_call | solution.py:499
  177.4 1.1 copy.16
  178.5 1.6 copy.17
  (1 shorter events, 0.0 us)

commit v5 on v3

--- a/solution.py
+++ b/solution.py
@@ -106,6 +106,10 @@
         before = (plane_down == plane) & (index < order)
         rank = jnp.sum(jnp.where(before, 1, 0), axis=0, keepdims=True)
         keys[1:2, :] = jnp.where(slot == 1, plane * nr + rank, -1)
+    else:
+        keys[1:2, :] = jnp.where(slot == 1, place, -1)
+
+    def relay_matrices():
         member = (owner // nf) * 2 + owner % 2 + 1
         wide = half * nr
         column = lax.broadcasted_iota(jnp.int32, (wide, mats), 0) % nr
@@ -118,8 +122,8 @@
         wanted = jnp.where(wanted, 1.0, 0.0)
         spread_in[...] = wanted.astype(BF)
         spread_out[...] = jnp.transpose(wanted).astype(BF)
-    else:
-        keys[1:2, :] = jnp.where(slot == 1, place, -1)
+
+    few = 2 if relayed else 1
 
     def select(s):
         places = nz * nr if relayed and s == 1 else mats
@@ -129,14 +133,16 @@
     def gather(s):
         chosen = select(s)
 
-        @pl.loop(0, half)
-        def _(a):
-            both = jnp.concatenate([g[a], g[a + half]], axis=0)
+        @pl.loop(0, half // 2, unroll=half // 2 if relayed else 1)
+        def _(k):
+            both = jnp.concatenate([g[2 * k], g[2 * k + half], g[2 * k + 1], g[2 * k + 1 + half]], axis=0)
             out = mm(chosen, both, ((1,), (1,))).astype(BF)
-            if relayed and s == 1:
-                zs_buf[:, a] = out.reshape(nz, nr, 128)
-            else:
-                s_buf[s, :, a] = out.reshape(nf, nr, 128)
+            for i in range(2):
+                part = out[:, 128 * i : 128 * i + 128]
+                if relayed and s == 1:
+                    zs_buf[:, 2 * k + i] = part.reshape(nz, nr, 128)
+                else:
+                    s_buf[s, :, 2 * k + i] = part.reshape(nf, nr, 128)
 
     def regroup_two(s, k):
         first, second = k, k + 1
@@ -148,7 +154,7 @@
         t_buf[s, pl.ds(second * nr, nr)] = out[:, 128:].reshape(nr, blk, 128).astype(BF)
 
     def regroup_all(s):
-        @pl.loop(0, nf // 2)
+        @pl.loop(0, nf // 2, unroll=few)
         def _(k):
             regroup_two(s, 2 * k)
 
@@ -214,35 +220,43 @@
                 total = total + jnp.sum(value * value, axis=0, keepdims=True)
             return total
 
-        total = lax.fori_loop(0, width // 128, start, jnp.zeros((1, 128), F32), unroll=2)
+        total = lax.fori_loop(0, width // 128, start, jnp.zeros((1, 128), F32), unroll=2 * few)
         scale = 1.0 / (jnp.sqrt(jnp.sum(total, axis=1, keepdims=True)) + 1e-07)
 
-        @pl.loop(0, width // 256)
+        @pl.loop(0, width // 256, unroll=few)
         def _(n):
             cols = tile_cols(n, 256)
             x[:, cols] = (nest[:, cols] * scale).astype(BF)
 
         @pl.loop(0, ITERS)
         def _(turn):
-            for n in range(pad // 256):
-                cols = slice(256 * n, 256 * n + 256)
+            def columns(count, step):
+                if relayed:
+                    for n in range(count):
+                        step(slice(256 * n, 256 * n + 256))
+                else:
+                    pl.loop(0, count)(lambda n: step(tile_cols(n, 256)))
+
+            def to_gram(cols):
                 gram[:, cols] = mm(x[...], x[cols, :], ((1,), (1,))).astype(BF)
 
-            for n in range(pad // 256):
-                cols = slice(256 * n, 256 * n + 256)
+            def to_mixed(cols):
                 part = gram[:, cols]
                 square = mm(gram[...], part)
                 mixed[:, cols] = (-4.775 * part.astype(F32) + 2.0315 * square).astype(BF)
 
-            for n in range(width // 256):
-                cols = slice(256 * n, 256 * n + 256)
+            def to_x(cols):
                 part = x[:, cols]
                 product = mm(mixed[...], part)
                 x[:, cols] = (3.4445 * part.astype(F32) + product).astype(BF)
 
+            columns(pad // 256, to_gram)
+            columns(pad // 256, to_mixed)
+            columns(width // 256, to_x)
+
         factor = 0.2 * max(hid, width) ** 0.5
 
-        @pl.loop(0, nr // 2, unroll=2)
+        @pl.loop(0, nr // 2, unroll=2 * few)
         def _(q):
             cols = tile_cols(q, 128)
             both = jnp.concatenate(
@@ -255,7 +269,7 @@
                 )
 
     def ungroup(s):
-        @pl.loop(0, nf // 2)
+        @pl.loop(0, nf // 2, unroll=few)
         def _(k):
             pair = jnp.concatenate(
                 [u_buf[s, pl.ds((2 * k + i) * nr, nr)].reshape(nr * blk, 128) for i in range(2)], axis=1
@@ -290,7 +304,7 @@
                 visit(2 * to_r + to_c, to_r, 2 * z + to_c)
 
     def relay_in():
-        @pl.loop(0, nz // 2)
+        @pl.loop(0, nz // 2, unroll=few)
         def _(k):
             pair = jnp.concatenate([zr_buf[2 * k + i].reshape(half * nr, 128) for i in range(2)], axis=1)
             out = mm(spread_in[...], pair)
@@ -319,7 +333,7 @@
         in_plane(send)
 
     def relay_out():
-        @pl.loop(0, nz // 2)
+        @pl.loop(0, nz // 2, unroll=few)
         def _(k):
             pair = jnp.concatenate(
                 [zv_buf[:, 2 * k + i].reshape(2 * nr * blk, 128) for i in range(2)], axis=1
@@ -329,14 +343,17 @@
                 zs_buf[2 * k + i] = out[:, 128 * i : 128 * i + 128].reshape(half, nr, 128)
 
     def unpack(second):
-        chosen = [select(0), select(1)]
-
-        @pl.loop(0, half)
-        def _(a):
-            first = mm(s_buf[0, :, a].reshape(mats, 128), chosen[0], ((0,), (0,)))
-            out = (first + mm(second(a), chosen[1], ((0,), (0,)))).astype(BF)
-            upd_ref[a] = out[0:64]
-            upd_ref[a + half] = out[64:128]
+        chosen = jnp.concatenate([select(0), select(1)], axis=0)
+
+        @pl.loop(0, half // 2, unroll=half // 2 if relayed else 1)
+        def _(k):
+            tiles = [
+                jnp.concatenate([s_buf[0, :, 2 * k + i].reshape(mats, 128), second(2 * k + i)], axis=0) for i in range(2)
+            ]
+            out = mm(jnp.concatenate(tiles, axis=1), chosen, ((0,), (0,))).astype(BF)
+            for i in range(2):
+                upd_ref[2 * k + i] = out[128 * i : 128 * i + 64]
+                upd_ref[2 * k + i + half] = out[128 * i + 64 : 128 * i + 128]
 
     def all_but_one(ref):
         return ref.at[pl.ds(0, ref.shape[0] - 1)]
@@ -350,6 +367,7 @@
         for load in loads[1:]:
             load.wait()
         regroup_all(0)
+        relay_matrices()
         spin_momentum(1)
         spin_momentum(0)
 

time: 157 us -> 152 us (0.968)
  Pallas kernels: 150 us -> 145 us
    pallas_call x1, Pallas kernels: 150 us -> 145 us  [run(): pl.pallas_call(functools.partial(kernel, cfg, relayed), out_shape=(jax.Sh...]
where the time goes in v5:
time: 152 us
  Pallas kernels  145 us (95%)
  local copies, waits for them, and re-layouts  2.68 us (2%)
  other arithmetic  2.54 us (2%)
    pallas_call x1, Pallas kernels, run(): pl.pallas_call(functools.partial(kernel, cfg, relayed), out_shape=(jax.Sh...  145 us

profile of v5, /device:TPU:1, one launch (start us, length us, event | category | flops | bytes accessed | tf_op | source)
XLA Modules:
  0.0 151.8 jit_solution(838315550024284627)
XLA Ops:
  0.6 0.7 and_select_fusion
  1.3 0.9 fusion
  2.2 0.3 convert_reduce_fusion
  2.5 0.6 reduce_max.9
  3.8 145.3 %conditional.1 = (bf16[44,64,256]{2,1,0:T(8,128)(2,1)S(1)}, bf16[1,2,704,1024]{3,2,1,0:T(8,128)(2,1)S(1)}) conditional(s32[]{:T(128)} %convert_element_type.7, (s32[256]{0:T(256)}, bf16[1,2,704,1024]{3,2,1,0:T(8,128)(2,1)}, bf16[44,64,256]{2,1,0:T(8,128)(2,1)}, bf16[384,352]{1,0:T(8,128)(2,1)}, bf16[352,384]{1,0:T(8,128)(2,1)}, ...), branch_computations={%region_2.3_spmd, %region_3.4_spmd} | conditional | bytes 16 | solution.py:511
  3.9 145.1 %muon_relayed.1 = (bf16[44,64,256]{2,1,0:T(8,128)(2,1)S(1)}, bf16[2,704,1024]{2,1,0:T(8,128)(2,1)S(1)}) custom-call(s32[1,256]{1,0:T(1,128)} %bitcast.16, bf16[44,64,256]{2,1,0:T(8,128)(2,1)} %get-tuple-element.52.g_hbm, bf16[2,704,1024]{2,1,0:T(8,128)(2,1)} %bitcast.9, bf16[384,352]{1,0:T(8,128)(2,1)} %get-tuple-element.54.regroup_hbm, ...), custom_call_target="tpu_custom_call" | custom-call | tf_op jit(solution)/shard_map/cond/branch_1_fun/muon_relayed/pallas_call | solution.py:475
  149.2 1.1 copy.16
  150.3 1.6 %copy.17 = bf16[1,2,704,1024]{3,2,1,0:T(8,128)(2,1)} copy(bf16[1,2,704,1024]{3,2,1,0:T(8,128)(2,1)S(1)} %get-tuple-element.74) | data formatting | bytes 5767168
  (1 shorter events, 0.0 us)

commit v6 on v5

--- a/solution.py
+++ b/solution.py
@@ -173,11 +173,11 @@
     def send_out(s):
         def send(to_r, to_f):
             pltpu.make_async_remote_copy(
-                w_buf.at[s, to_r * nf + lax.rem(to_f, 2) * nz + to_f // 2], u_buf.at[s, fs * nr + rep], out_send.at[s], out_recv.at[s],
+                w_buf.at[s, to_r * nf + lax.rem(to_f, 2) * nz + to_f // 2], u_buf.at[s, fs * nr + rep], out_send.at[s], out_recv.at[s, z],
                 device_id=(to_r, to_f), device_id_type=MESH,
             ).start()
 
-        pltpu.make_async_copy(w_buf.at[s, lane], u_buf.at[s, fs * nr + rep], out_recv.at[s]).start()
+        pltpu.make_async_copy(w_buf.at[s, lane], u_buf.at[s, fs * nr + rep], out_recv.at[s, z]).start()
         everyone(send)
 
     def spin_momentum(s):
@@ -203,7 +203,7 @@
 
         pltpu.make_async_copy(new.at[s], new_hbm.at[s], new_sem.at[s]).start()
 
-    def orthogonalize(s):
+    def orthogonalize(s, before_last=None):
         def start(q, total):
             pair = jnp.concatenate(
                 [v_buf[s, pl.ds((2 * q + i) * nf, nf)].reshape(upper, 128) for i in range(2)], axis=1
@@ -252,6 +252,8 @@
 
             columns(pad // 256, to_gram)
             columns(pad // 256, to_mixed)
+            if before_last is not None:
+                pl.when(turn == ITERS - 1)(before_last)
             columns(width // 256, to_x)
 
         factor = 0.2 * max(hid, width) ** 0.5
@@ -269,14 +271,24 @@
                 )
 
     def ungroup(s):
-        @pl.loop(0, nf // 2, unroll=few)
-        def _(k):
+        def one(dz):
+            k = lax.rem(z + dz, nz)
+            wait_bytes(u_buf.at[s, pl.ds(2 * k * nr, 2 * nr)], out_recv.at[s, k])
             pair = jnp.concatenate(
                 [u_buf[s, pl.ds((2 * k + i) * nr, nr)].reshape(nr * blk, 128) for i in range(2)], axis=1
             )
             out = mm(regroup_t[...], pair).astype(BF)
             s_buf[s, 2 * k] = out[:, :128].reshape(half, nr, 128)
             s_buf[s, 2 * k + 1] = out[:, 128:].reshape(half, nr, 128)
+
+        @pl.loop(0, nz // 2 - 1)
+        def _(k):
+            one(k + 1)
+            one(nz - 1 - k)
+
+        @pl.loop(0, 2)
+        def _(k):
+            one(k * (nz // 2))
 
     def along_z(src, dst, send_sem, recv_sem):
         pltpu.make_async_copy(src.at[z], dst.at[z], recv_sem).start()
@@ -379,17 +391,17 @@
         plane_out()
 
         wait_bytes(v_buf.at[0], in_recv.at[0])
-        orthogonalize(0)
+
+        def second_back():
+            wait_bytes(zv_buf, po_recv)
+            wait_bytes(all_but_one(zs_buf), z_send)
+            relay_out()
+            along_z(zs_buf, zu_buf, zo_send, zo_recv)
+
+        orthogonalize(0, second_back)
         send_out(0)
-
-        wait_bytes(zv_buf, po_recv)
-        wait_bytes(all_but_one(zs_buf), z_send)
-        relay_out()
-        along_z(zs_buf, zu_buf, zo_send, zo_recv)
         store_momentum(1)
         store_momentum(0)
-
-        wait_bytes(u_buf.at[0], out_recv.at[0])
         ungroup(0)
         wait_bytes(zu_buf, zo_recv)
         unpack(lambda a: zu_buf[:, a].reshape(nz * nr, 128))
@@ -413,7 +425,6 @@
         for s in range(2):
             store_momentum(s)
         for s in range(2):
-            wait_bytes(u_buf.at[s], out_recv.at[s])
             ungroup(s)
         unpack(lambda a: s_buf[1, :, a].reshape(mats, 128))
 
@@ -493,7 +504,8 @@
                 pltpu.VMEM((pad, pad), BF),
                 pltpu.VMEM((pad, pad), BF),
                 pltpu.SemaphoreType.DMA((6,)),
-                *[pltpu.SemaphoreType.DMA((2,)) for _ in range(6)],
+                *[pltpu.SemaphoreType.DMA((2,)) for _ in range(5)],
+                pltpu.SemaphoreType.DMA((2, nz)),
                 *(relay_scratch if relayed else []),
             ],
             compiler_params=pltpu.CompilerParams(

time: 152 us -> 168 us (1.11)
  Pallas kernels: 145 us -> 161 us
    pallas_call x1, Pallas kernels: 145 us -> 161 us  [run(): pl.pallas_call(functools.partial(kernel, cfg, relayed), out_shape=(jax.Sh...]
where the time goes in v6:
time: 168 us
  Pallas kernels  161 us (96%)
  local copies, waits for them, and re-layouts  2.68 us (2%)
  other arithmetic  2.54 us (2%)
    pallas_call x1, Pallas kernels, run(): pl.pallas_call(functools.partial(kernel, cfg, relayed), out_shape=(jax.Sh...  161 us

profile of v6, /device:TPU:1, one launch (start us, length us, event | category | flops | bytes accessed | tf_op | source)
XLA Modules:
  0.0 168.1 jit_solution(5596721998456163303)
XLA Ops:
  0.6 0.7 and_select_fusion
  1.3 0.9 fusion
  2.2 0.3 convert_reduce_fusion
  2.5 0.6 reduce_max.9
  3.8 161.6 %conditional.1 = (bf16[44,64,256]{2,1,0:T(8,128)(2,1)S(1)}, bf16[1,2,704,1024]{3,2,1,0:T(8,128)(2,1)S(1)}) conditional(s32[]{:T(128)} %convert_element_type.7, (s32[256]{0:T(256)}, bf16[1,2,704,1024]{3,2,1,0:T(8,128)(2,1)}, bf16[44,64,256]{2,1,0:T(8,128)(2,1)}, bf16[384,352]{1,0:T(8,128)(2,1)}, bf16[352,384]{1,0:T(8,128)(2,1)}, ...), branch_computations={%region_2.3_spmd, %region_3.4_spmd} | conditional | bytes 16 | solution.py:523
  4.0 161.2 %muon_relayed.1 = (bf16[44,64,256]{2,1,0:T(8,128)(2,1)S(1)}, bf16[2,704,1024]{2,1,0:T(8,128)(2,1)S(1)}) custom-call(s32[1,256]{1,0:T(1,128)} %bitcast.16, bf16[44,64,256]{2,1,0:T(8,128)(2,1)} %get-tuple-element.52.g_hbm, bf16[2,704,1024]{2,1,0:T(8,128)(2,1)} %bitcast.9, bf16[384,352]{1,0:T(8,128)(2,1)} %get-tuple-element.54.regroup_hbm, ...), custom_call_target="tpu_custom_call" | custom-call | tf_op jit(solution)/shard_map/cond/branch_1_fun/muon_relayed/pallas_call | solution.py:486
  165.4 1.1 copy.16
  166.5 1.6 copy.17
  (1 shorter events, 0.0 us)

commit v7 on v6

--- a/solution.py
+++ b/solution.py
@@ -64,15 +64,27 @@
     def faces(dz, dc):
         return 2 * lax.rem(z + dz, nz) + lax.rem(core + dc, 2)
 
-    def everyone(visit):
-        @pl.loop(0, nz // 2 - 1)
+    def everyone(visit, beside=None):
+        def four(k, j):
+            to_r = moved(j)
+            for dc in range(2):
+                visit(to_r, faces(k + 1, dc))
+                visit(to_r, faces(nz - 1 - k, dc))
+
+        done = 0
+        if beside is not None:
+            done = 2
+            for k in range(done):
+                @pl.loop(0, nr)
+                def _(j):
+                    beside(k * nr + j)
+                    four(k, j)
+
+        @pl.loop(done, nz // 2 - 1)
         def _(k):
             @pl.loop(0, nr)
             def _(j):
-                to_r = moved(j)
-                for dc in range(2):
-                    visit(to_r, faces(k + 1, dc))
-                    visit(to_r, faces(nz - 1 - k, dc))
+                four(k, j)
 
         for dc in range(2):
             visit(rep, faces(nz // 2, dc))
@@ -158,7 +170,7 @@
         def _(k):
             regroup_two(s, 2 * k)
 
-    def send_in(s, regrouped):
+    def send_in(s, regrouped, beside=None):
         def send(to_r, to_f):
             pltpu.make_async_remote_copy(
                 t_buf.at[s, to_f * nr + to_r], v_buf.at[s, lane], in_send.at[s], in_recv.at[s],
@@ -168,7 +180,7 @@
         if not regrouped:
             regroup_all(s)
         pltpu.make_async_copy(t_buf.at[s, fs * nr + rep], v_buf.at[s, lane], in_recv.at[s]).start()
-        everyone(send)
+        everyone(send, beside)
 
     def send_out(s):
         def send(to_r, to_f):
@@ -203,7 +215,7 @@
 
         pltpu.make_async_copy(new.at[s], new_hbm.at[s], new_sem.at[s]).start()
 
-    def orthogonalize(s, before_last=None):
+    def orthogonalize(s):
         def start(q, total):
             pair = jnp.concatenate(
                 [v_buf[s, pl.ds((2 * q + i) * nf, nf)].reshape(upper, 128) for i in range(2)], axis=1
@@ -252,8 +264,6 @@
 
             columns(pad // 256, to_gram)
             columns(pad // 256, to_mixed)
-            if before_last is not None:
-                pl.when(turn == ITERS - 1)(before_last)
             columns(width // 256, to_x)
 
         factor = 0.2 * max(hid, width) ** 0.5
@@ -323,16 +333,22 @@
             for i in range(2):
                 zt_buf[:, 2 * k + i] = out[:, 128 * i : 128 * i + 128].reshape(2 * nr, blk, 128).astype(BF)
 
-        def send(to, to_r, to_f):
+    def send_in_plane(t):
+        to_r = moved(t // 2)
+        to_c = lax.rem(core + t, 2)
+
+        @pl.when(t > 0)
+        def _():
             pltpu.make_async_remote_copy(
-                zt_buf.at[to], v_buf.at[1, pl.ds(rep * nf + core * nz, nz)], p_send, in_recv.at[1],
-                device_id=(to_r, to_f), device_id_type=MESH,
+                zt_buf.at[2 * to_r + to_c], v_buf.at[1, pl.ds(rep * nf + core * nz, nz)], p_send, in_recv.at[1],
+                device_id=(to_r, 2 * z + to_c), device_id_type=MESH,
             ).start()
 
-        pltpu.make_async_copy(
-            zt_buf.at[2 * rep + core], v_buf.at[1, pl.ds(rep * nf + core * nz, nz)], in_recv.at[1]
-        ).start()
-        in_plane(send)
+        @pl.when(t == 0)
+        def _():
+            pltpu.make_async_copy(
+                zt_buf.at[2 * rep + core], v_buf.at[1, pl.ds(rep * nf + core * nz, nz)], in_recv.at[1]
+            ).start()
 
     def plane_out():
         def send(to, to_r, to_f):
@@ -385,23 +401,22 @@
 
         wait_bytes(zr_buf, z_recv)
         relay_in()
-        send_in(0, True)
+        send_in(0, True, send_in_plane)
         wait_bytes(v_buf.at[1], in_recv.at[1])
         orthogonalize(1)
         plane_out()
 
         wait_bytes(v_buf.at[0], in_recv.at[0])
-
-        def second_back():
-            wait_bytes(zv_buf, po_recv)
-            wait_bytes(all_but_one(zs_buf), z_send)
-            relay_out()
-            along_z(zs_buf, zu_buf, zo_send, zo_recv)
-
-        orthogonalize(0, second_back)
+        orthogonalize(0)
         send_out(0)
+
+        wait_bytes(zv_buf, po_recv)
+        wait_bytes(all_but_one(zs_buf), z_send)
+        relay_out()
+        along_z(zs_buf, zu_buf, zo_send, zo_recv)
         store_momentum(1)
         store_momentum(0)
+
         ungroup(0)
         wait_bytes(zu_buf, zo_recv)
         unpack(lambda a: zu_buf[:, a].reshape(nz * nr, 128))

time: 168 us -> 152 us (0.905)
  Pallas kernels: 161 us -> 145 us
    pallas_call x1, Pallas kernels: 161 us -> 145 us  [run(): pl.pallas_call(functools.partial(kernel, cfg, relayed), out_shape=(jax.Sh...]
where the time goes in v7:
time: 152 us
  Pallas kernels  145 us (95%)
  local copies, waits for them, and re-layouts  2.68 us (2%)
  other arithmetic  2.54 us (2%)
    pallas_call x1, Pallas kernels, run(): pl.pallas_call(functools.partial(kernel, cfg, relayed), out_shape=(jax.Sh...  145 us

profile of v7, /device:TPU:1, one launch (start us, length us, event | category | flops | bytes accessed | tf_op | source)
XLA Modules:
  0.0 152.1 jit_solution(4812256939706823156)
XLA Ops:
  0.6 0.7 and_select_fusion
  1.3 0.9 fusion
  2.2 0.3 convert_reduce_fusion
  2.5 0.6 reduce_max.9
  3.8 145.6 %conditional.1 = (bf16[44,64,256]{2,1,0:T(8,128)(2,1)S(1)}, bf16[1,2,704,1024]{3,2,1,0:T(8,128)(2,1)S(1)}) conditional(s32[]{:T(128)} %convert_element_type.7, (s32[256]{0:T(256)}, bf16[1,2,704,1024]{3,2,1,0:T(8,128)(2,1)}, bf16[44,64,256]{2,1,0:T(8,128)(2,1)}, bf16[384,352]{1,0:T(8,128)(2,1)}, bf16[352,384]{1,0:T(8,128)(2,1)}, ...), branch_computations={%region_2.3_spmd, %region_3.4_spmd} | conditional | bytes 16 | solution.py:538
  3.9 145.3 %muon_relayed.1 = (bf16[44,64,256]{2,1,0:T(8,128)(2,1)S(1)}, bf16[2,704,1024]{2,1,0:T(8,128)(2,1)S(1)}) custom-call(s32[1,256]{1,0:T(1,128)} %bitcast.16, bf16[44,64,256]{2,1,0:T(8,128)(2,1)} %get-tuple-element.52.g_hbm, bf16[2,704,1024]{2,1,0:T(8,128)(2,1)} %bitcast.9, bf16[384,352]{1,0:T(8,128)(2,1)} %get-tuple-element.54.regroup_hbm, ...), custom_call_target="tpu_custom_call" | custom-call | tf_op jit(solution)/shard_map/cond/branch_1_fun/muon_relayed/pallas_call | solution.py:501
  149.4 1.1 copy.16
  150.5 1.6 %copy.17 = bf16[1,2,704,1024]{3,2,1,0:T(8,128)(2,1)} copy(bf16[1,2,704,1024]{3,2,1,0:T(8,128)(2,1)S(1)} %get-tuple-element.74) | data formatting | bytes 5767168
  (1 shorter events, 0.0 us)

commit v8 on v7

--- a/solution.py
+++ b/solution.py
@@ -64,23 +64,14 @@
     def faces(dz, dc):
         return 2 * lax.rem(z + dz, nz) + lax.rem(core + dc, 2)
 
-    def everyone(visit, beside=None):
+    def everyone(visit):
         def four(k, j):
             to_r = moved(j)
             for dc in range(2):
                 visit(to_r, faces(k + 1, dc))
                 visit(to_r, faces(nz - 1 - k, dc))
 
-        done = 0
-        if beside is not None:
-            done = 2
-            for k in range(done):
-                @pl.loop(0, nr)
-                def _(j):
-                    beside(k * nr + j)
-                    four(k, j)
-
-        @pl.loop(done, nz // 2 - 1)
+        @pl.loop(0, nz // 2 - 1)
         def _(k):
             @pl.loop(0, nr)
             def _(j):
@@ -170,7 +161,7 @@
         def _(k):
             regroup_two(s, 2 * k)
 
-    def send_in(s, regrouped, beside=None):
+    def send_in(s, regrouped):
         def send(to_r, to_f):
             pltpu.make_async_remote_copy(
                 t_buf.at[s, to_f * nr + to_r], v_buf.at[s, lane], in_send.at[s], in_recv.at[s],
@@ -180,7 +171,7 @@
         if not regrouped:
             regroup_all(s)
         pltpu.make_async_copy(t_buf.at[s, fs * nr + rep], v_buf.at[s, lane], in_recv.at[s]).start()
-        everyone(send, beside)
+        everyone(send)
 
     def send_out(s):
         def send(to_r, to_f):
@@ -249,13 +240,25 @@
                 else:
                     pl.loop(0, count)(lambda n: step(tile_cols(n, 256)))
 
+            def mirror(ref, cols, part):
+                lines = slice(cols.start, pad)
+                ref[lines, cols] = part.astype(BF)
+                if cols.stop < pad:
+                    ref[cols, cols.stop : pad] = jnp.transpose(part[256:]).astype(BF)
+
             def to_gram(cols):
-                gram[:, cols] = mm(x[...], x[cols, :], ((1,), (1,))).astype(BF)
+                if relayed:
+                    mirror(gram, cols, mm(x[cols.start :, :], x[cols, :], ((1,), (1,))))
+                else:
+                    gram[:, cols] = mm(x[...], x[cols, :], ((1,), (1,))).astype(BF)
 
             def to_mixed(cols):
-                part = gram[:, cols]
-                square = mm(gram[...], part)
-                mixed[:, cols] = (-4.775 * part.astype(F32) + 2.0315 * square).astype(BF)
+                lines = slice(cols.start if relayed else 0, pad)
+                part = -4.775 * gram[lines, cols].astype(F32) + 2.0315 * mm(gram[lines, :], gram[:, cols])
+                if relayed:
+                    mirror(mixed, cols, part)
+                else:
+                    mixed[:, cols] = part.astype(BF)
 
             def to_x(cols):
                 part = x[:, cols]
@@ -336,18 +339,13 @@
     def send_in_plane(t):
         to_r = moved(t // 2)
         to_c = lax.rem(core + t, 2)
-
-        @pl.when(t > 0)
-        def _():
+        landing = v_buf.at[1, pl.ds(rep * nf + core * nz, nz)]
+        if isinstance(t, int):
+            pltpu.make_async_copy(zt_buf.at[2 * rep + core], landing, in_recv.at[1]).start()
+        else:
             pltpu.make_async_remote_copy(
-                zt_buf.at[2 * to_r + to_c], v_buf.at[1, pl.ds(rep * nf + core * nz, nz)], p_send, in_recv.at[1],
+                zt_buf.at[2 * to_r + to_c], landing, p_send, in_recv.at[1],
                 device_id=(to_r, 2 * z + to_c), device_id_type=MESH,
-            ).start()
-
-        @pl.when(t == 0)
-        def _():
-            pltpu.make_async_copy(
-                zt_buf.at[2 * rep + core], v_buf.at[1, pl.ds(rep * nf + core * nz, nz)], in_recv.at[1]
             ).start()
 
     def plane_out():
@@ -401,7 +399,13 @@
 
         wait_bytes(zr_buf, z_recv)
         relay_in()
-        send_in(0, True, send_in_plane)
+        send_in_plane(0)
+
+        @pl.loop(1, 2 * nr)
+        def _(t):
+            send_in_plane(t)
+
+        send_in(0, True)
         wait_bytes(v_buf.at[1], in_recv.at[1])
         orthogonalize(1)
         plane_out()

time: 152 us -> 150 us (0.987)
  Pallas kernels: 145 us -> 143 us
    pallas_call x1, Pallas kernels: 145 us -> 143 us  [run(): pl.pallas_call(functools.partial(kernel, cfg, relayed), out_shape=(jax.Sh...]
where the time goes in v8:
time: 150 us
  Pallas kernels  143 us (95%)
  local copies, waits for them, and re-layouts  2.68 us (2%)
  other arithmetic  2.54 us (2%)
    pallas_call x1, Pallas kernels, run(): pl.pallas_call(functools.partial(kernel, cfg, relayed), out_shape=(jax.Sh...  143 us

profile of v8, /device:TPU:1, one launch (start us, length us, event | category | flops | bytes accessed | tf_op | source)
XLA Modules:
  0.0 149.6 jit_solution(9782899864739046399)
XLA Ops:
  0.6 0.7 and_select_fusion
  1.3 0.9 fusion
  2.2 0.3 convert_reduce_fusion
  2.5 0.6 reduce_max.9
  3.8 143.1 %conditional.1 = (bf16[44,64,256]{2,1,0:T(8,128)(2,1)S(1)}, bf16[1,2,704,1024]{3,2,1,0:T(8,128)(2,1)S(1)}) conditional(s32[]{:T(128)} %convert_element_type.7, (s32[256]{0:T(256)}, bf16[1,2,704,1024]{3,2,1,0:T(8,128)(2,1)}, bf16[44,64,256]{2,1,0:T(8,128)(2,1)}, bf16[384,352]{1,0:T(8,128)(2,1)}, bf16[352,384]{1,0:T(8,128)(2,1)}, ...), branch_computations={%region_2.3_spmd, %region_3.4_spmd} | conditional | bytes 16 | solution.py:542
  4.0 142.7 %muon_relayed.1 = (bf16[44,64,256]{2,1,0:T(8,128)(2,1)S(1)}, bf16[2,704,1024]{2,1,0:T(8,128)(2,1)S(1)}) custom-call(s32[1,256]{1,0:T(1,128)} %bitcast.16, bf16[44,64,256]{2,1,0:T(8,128)(2,1)} %get-tuple-element.52.g_hbm, bf16[2,704,1024]{2,1,0:T(8,128)(2,1)} %bitcast.9, bf16[384,352]{1,0:T(8,128)(2,1)} %get-tuple-element.54.regroup_hbm, ...), custom_call_target="tpu_custom_call" | custom-call | tf_op jit(solution)/shard_map/cond/branch_1_fun/muon_relayed/pallas_call | solution.py:505
  147.0 1.1 copy.16
  148.1 1.6 %copy.17 = bf16[1,2,704,1024]{3,2,1,0:T(8,128)(2,1)} copy(bf16[1,2,704,1024]{3,2,1,0:T(8,128)(2,1)S(1)} %get-tuple-element.74) | data formatting | bytes 5767168
  (1 shorter events, 0.0 us)

commit v9 on v8

--- a/solution.py
+++ b/solution.py
@@ -126,7 +126,7 @@
         spread_in[...] = wanted.astype(BF)
         spread_out[...] = jnp.transpose(wanted).astype(BF)
 
-    few = 2 if relayed else 1
+    few = 4 if relayed else 1
 
     def select(s):
         places = nz * nr if relayed and s == 1 else mats

time: 150 us -> 149 us (level)
  no operation moved by 1% of the time
where the time goes in v9:
time: 149 us
  Pallas kernels  142 us (95%)
  local copies, waits for them, and re-layouts  2.68 us (2%)
  other arithmetic  2.54 us (2%)
    pallas_call x1, Pallas kernels, run(): pl.pallas_call(functools.partial(kernel, cfg, relayed), out_shape=(jax.Sh...  142 us

profile of v9, /device:TPU:1, one launch (start us, length us, event | category | flops | bytes accessed | tf_op | source)
XLA Modules:
  0.0 148.6 jit_solution(6149708234546188101)
XLA Ops:
  0.6 0.7 and_select_fusion
  1.3 0.9 fusion
  2.2 0.3 convert_reduce_fusion
  2.5 0.6 reduce_max.9
  3.8 142.1 %conditional.1 = (bf16[44,64,256]{2,1,0:T(8,128)(2,1)S(1)}, bf16[1,2,704,1024]{3,2,1,0:T(8,128)(2,1)S(1)}) conditional(s32[]{:T(128)} %convert_element_type.7, (s32[256]{0:T(256)}, bf16[1,2,704,1024]{3,2,1,0:T(8,128)(2,1)}, bf16[44,64,256]{2,1,0:T(8,128)(2,1)}, bf16[384,352]{1,0:T(8,128)(2,1)}, bf16[352,384]{1,0:T(8,128)(2,1)}, ...), branch_computations={%region_2.3_spmd, %region_3.4_spmd} | conditional | bytes 16 | solution.py:542
  4.0 141.7 %muon_relayed.1 = (bf16[44,64,256]{2,1,0:T(8,128)(2,1)S(1)}, bf16[2,704,1024]{2,1,0:T(8,128)(2,1)S(1)}) custom-call(s32[1,256]{1,0:T(1,128)} %bitcast.16, bf16[44,64,256]{2,1,0:T(8,128)(2,1)} %get-tuple-element.52.g_hbm, bf16[2,704,1024]{2,1,0:T(8,128)(2,1)} %bitcast.9, bf16[384,352]{1,0:T(8,128)(2,1)} %get-tuple-element.54.regroup_hbm, ...), custom_call_target="tpu_custom_call" | custom-call | tf_op jit(solution)/shard_map/cond/branch_1_fun/muon_relayed/pallas_call | solution.py:505
  146.0 1.1 copy.16
  147.1 1.6 %copy.17 = bf16[1,2,704,1024]{3,2,1,0:T(8,128)(2,1)} copy(bf16[1,2,704,1024]{3,2,1,0:T(8,128)(2,1)S(1)} %get-tuple-element.74) | data formatting | bytes 5767168
  (1 shorter events, 0.0 us)
